TPU v7x, 512 devices: a whole 4x4x16 slice. The times are simulated.
512 devices in a mesh: wide: 128 (over z, x, core), narrow: 4 (over y).
Axes of the slice: x: 4, y: 4, z: 16, core: 2. Of those that a mesh axis runs over, the one named last changes fastest.
Arguments:
- features: bfloat16 [128, 4, 512, 128], P('wide', 'narrow'), may hold values from -6 to 6
- send_rows: int32 [128, 4, 128, 2], P('wide', 'narrow'), may hold values from 0 to 511
- send_counts: int32 [128, 4, 128], P('wide', 'narrow'), may hold values from 1 to 2, as said below
- tile_index: int32 [128, 4, 4, 3], P('wide', 'narrow'), may hold values from 0 to 5, as said below
- tile_weight: bfloat16 [128, 4, 4, 3, 128, 128], P('wide', 'narrow'), may hold values from -0.3125 to 0.3125
- first_layer_self_weight: bfloat16 [128, 256], replicated, may hold values from -0.5 to 0.5
- first_layer_neighbour_weight: bfloat16 [128, 256], replicated, may hold values from -0.5 to 0.5
- layer1_bias: float32 [256], replicated, may hold values from -3 to 3
- layer2_self: bfloat16 [256, 172], replicated, may hold values from -0.375 to 0.375
- layer2_neigh: bfloat16 [256, 172], replicated, may hold values from -0.375 to 0.375
- grad_logits: bfloat16 [128, 4, 512, 172], P('wide', 'narrow'), may hold values from -0.01171875 to 0.01171875
Outputs:
- logits: bfloat16 [128, 4, 512, 172], P('wide', 'narrow')
- first_self_weight_gradient: float32 [128, 256], replicated
- first_neighbour_weight_gradient: float32 [128, 256], replicated
- grad_bias1: float32 [256], replicated
- grad_self2: float32 [256, 172], replicated
- grad_neigh2: float32 [256, 172], replicated
Inputs may be any that keep to these rules, and one draw needn't show every extreme that they name: `send_counts`: every sub-partition fills all 2 slots toward at least one peer. `tile_index`: indices count 128-row blocks of the extended rows (own rows, then received rows). Tile 0 of block b is the own block b; tile 1 is a received block, and every received block is read by some tile of the sub-partition.
All inputs are finite; a program needn't handle non-finite values.
Results may differ from a plain program's by a relative error of at most 0.015.
The roundings to bfloat16 on the way count: a program that leaves them out, or rounds other values in their place, can miss the bound.
Values may be sent and summed in bfloat16 or wider, within the bound.
No kernel may reach another device: no remote copies, remote signals or barrier semaphores. Data moves between devices by JAX's collectives and lax.ppermute only.
A program may use at most 64 MiB of HBM per device.

v0:
```python
import jax
import jax.numpy as jnp
from jax import lax
from jax.sharding import PartitionSpec as P


def aggregate(tile_weight, tile_index, extended):
    columns = extended.shape[-1]
    blocks = extended.reshape(-1, 128, columns)
    picked = blocks[tile_index]
    summed = jnp.einsum("bkij,bkjf->bif", tile_weight, picked, preferred_element_type=jnp.float32)
    return summed.reshape(-1, columns)


def split_parts(values):
    upper = values.astype(jnp.bfloat16)
    lower = (values - upper.astype(jnp.float32)).astype(jnp.bfloat16)
    return (upper, lower)


def spread_back(tile_weight, tile_index, grads, ext_blocks):
    columns = grads.shape[-1]
    row_blocks = tile_index.shape[0]
    shaped = grads.reshape(row_blocks, 128, columns)
    upper, lower = split_parts(shaped)
    contrib = jnp.einsum("bkij,bif->bkjf", tile_weight, upper, preferred_element_type=jnp.float32)
    contrib = contrib + jnp.einsum(
        "bkij,bif->bkjf", tile_weight, lower, preferred_element_type=jnp.float32
    )
    onehot = (
        tile_index.reshape(-1)[:, None] == jnp.arange(ext_blocks, dtype=jnp.int32)[None, :]
    ).astype(jnp.float32)
    flat = contrib.reshape(onehot.shape[0], -1)
    summed = jnp.dot(onehot.T, flat, precision=lax.Precision.HIGHEST)
    return summed.reshape(ext_blocks * 128, columns)


def shards(
    features,
    send_rows,
    send_counts,
    tile_index,
    tile_weight,
    first_layer_self_weight,
    first_layer_neighbour_weight,
    layer1_bias,
    layer2_self,
    layer2_neigh,
    grad_logits,
):
    local_feat = features[0, 0]
    local_rows = send_rows[0, 0]
    local_counts = send_counts[0, 0]
    local_index = tile_index[0, 0]
    local_tiles = tile_weight[0, 0]
    local_grad = grad_logits[0, 0]
    num_rows = local_feat.shape[0]
    peers = local_rows.shape[0]
    slots = local_rows.shape[1]
    ext_blocks = (num_rows + peers * slots) // 128
    live_slot = jnp.arange(slots, dtype=jnp.int32)[None, :] < local_counts[:, None]
    flat_send = local_rows.reshape(-1)
    flat_live = live_slot.reshape(-1)

    def outgoing(table):
        picked = table[local_rows]
        return jnp.where(live_slot[..., None], picked, jnp.zeros((), table.dtype))

    halo_feat = lax.all_to_all(
        outgoing(local_feat), "wide", split_axis=0, concat_axis=0, tiled=True
    )
    ext_feat = jnp.concatenate([local_feat, halo_feat.reshape(-1, local_feat.shape[1])], axis=0)
    neighbour_feature_sum = aggregate(local_tiles, local_index, ext_feat).astype(jnp.bfloat16)
    preactivation_values = jnp.dot(
        local_feat, first_layer_self_weight, preferred_element_type=jnp.float32
    )
    preactivation_values = (
        preactivation_values
        + jnp.dot(
            neighbour_feature_sum, first_layer_neighbour_weight, preferred_element_type=jnp.float32
        )
        + layer1_bias
    )
    hidden = jnp.maximum(preactivation_values, 0.0).astype(jnp.bfloat16)
    halo_hid = lax.all_to_all(outgoing(hidden), "wide", split_axis=0, concat_axis=0, tiled=True)
    ext_hid = jnp.concatenate([hidden, halo_hid.reshape(-1, hidden.shape[1])], axis=0)
    agg_hidden = aggregate(local_tiles, local_index, ext_hid).astype(jnp.bfloat16)
    scores = jnp.dot(hidden, layer2_self, preferred_element_type=jnp.float32)
    scores = scores + jnp.dot(agg_hidden, layer2_neigh, preferred_element_type=jnp.float32)
    logits = scores.astype(jnp.bfloat16)
    grad_self2 = jnp.dot(hidden.T, local_grad, preferred_element_type=jnp.float32)
    grad_neigh2 = jnp.dot(agg_hidden.T, local_grad, preferred_element_type=jnp.float32)
    grad_hidden = jnp.dot(local_grad, layer2_self.T, preferred_element_type=jnp.float32)
    grad_agg = jnp.dot(local_grad, layer2_neigh.T, preferred_element_type=jnp.float32)
    grad_ext = spread_back(local_tiles, local_index, grad_agg, ext_blocks)
    outbound = grad_ext[num_rows:].reshape(peers, slots, grad_ext.shape[1])
    returned_rows = lax.all_to_all(
        outbound.astype(jnp.bfloat16), "wide", split_axis=0, concat_axis=0, tiled=True
    ).astype(outbound.dtype)
    values = returned_rows.reshape(-1, returned_rows.shape[-1])
    values = jnp.where(flat_live[:, None], values, jnp.zeros((), values.dtype))
    empty = jnp.zeros((num_rows, values.shape[-1]), jnp.float32)
    grad_hidden = grad_hidden + grad_ext[:num_rows] + empty.at[flat_send].add(values)
    grad_pre = jnp.where(preactivation_values > 0, grad_hidden, jnp.zeros((), jnp.float32)).astype(
        jnp.bfloat16
    )
    first_self_weight_gradient = jnp.dot(local_feat.T, grad_pre, preferred_element_type=jnp.float32)
    first_neighbour_weight_gradient = jnp.dot(
        neighbour_feature_sum.T, grad_pre, preferred_element_type=jnp.float32
    )
    grad_bias1 = jnp.sum(grad_pre.astype(jnp.float32), axis=0)
    summed = lax.psum(
        (
            first_self_weight_gradient,
            first_neighbour_weight_gradient,
            grad_bias1,
            grad_self2,
            grad_neigh2,
        ),
        ("wide", "narrow"),
    )
    return (logits[None, None], summed[0], summed[1], summed[2], summed[3], summed[4])


def solution(mesh):
    return jax.shard_map(
        shards,
        mesh=mesh,
        in_specs=(
            P("wide", "narrow", None, None),
            P("wide", "narrow", None, None),
            P("wide", "narrow", None),
            P("wide", "narrow", None, None),
            P("wide", "narrow", None, None, None, None),
            P(),
            P(),
            P(),
            P(),
            P(),
            P("wide", "narrow", None, None),
        ),
        out_specs=(P("wide", "narrow", None, None), P(), P(), P(), P(), P()),
        check_vma=False,
    )
```

profile of v0, /device:TPU:1, one launch (start us, length us, event | category | flops | bytes accessed | tf_op | source)
XLA Modules:
  0.0 570.4 jit_solution(8576476744068893793)
XLA Ops:
  9.0 1.7 gather_fusion
  11.5 20.4 %all-to-all-start = ((bf16[128,2,128]{2,1,0:T(2,128)(2,1)}), bf16[128,2,128]{2,1,0:T(2,128)(2,1)S(1)}, u32[]{:S(2)}, u32[]{:S(2)}) async-start(bf16[128,2,128]{2,1,0:T(2,128)(2,1)} %broadcast_select_fusion.1), calls=%async_computation | async-start | bytes 131072 | tf_op jit(solution)/shard_map/all_to_all | solution.py:69
  34.5 1.0 dot_general.56
  36.8 1.6 copy.29
  38.5 1.6 pad.8
  40.1 1.2 copy.40
  44.0 2.6 all-to-all-done
  46.7 13.5 %all-to-all-start.2 = ((bf16[128,2,256]{2,1,0:T(2,128)(2,1)}), bf16[128,2,256]{2,1,0:T(2,128)(2,1)S(1)}, u32[]{:S(2)}, u32[]{:S(2)}) async-start(bf16[128,2,256]{2,1,0:T(2,128)(2,1)} %convert_element_type.58), calls=%async_computation.2 | async-start | bytes 262144 | tf_op jit(solution)/shard_map/all_to_all | solution.py:97
  61.4 1.2 gather_fusion.2
  62.6 0.9 broadcast_select_fusion
  63.5 0.9 fusion.17
  64.3 11.9 %all-to-all-done.2 = bf16[128,2,256]{2,1,0:T(2,128)(2,1)S(1)} async-done(((bf16[128,2,256]{2,1,0:T(2,128)(2,1)}), bf16[128,2,256]{2,1,0:T(2,128)(2,1)S(1)}, u32[]{:S(2)}, u32[]{:S(2)}) %all-to-all-start.2) | async-done | bytes 131104 | tf_op jit(solution)/shard_map/all_to_all | solution.py:97
  76.2 7.2 %all-to-all-start.1 = ((bf16[128,2,256]{2,1,0:T(2,128)(2,1)}), bf16[128,2,256]{2,1,0:T(2,128)(2,1)S(1)}, u32[]{:S(2)}, u32[]{:S(2)}) async-start(bf16[128,2,256]{2,1,0:T(2,128)(2,1)} %broadcast_select_fusion), calls=%async_computation.1 | async-start | bytes 262144 | tf_op jit(solution)/shard_map/all_to_all | solution.py:85
  83.5 2.3 scatter_custom_fusion
  86.8 0.9 convolution_bitcast_fusion.2
  87.7 11.8 %all-to-all-done.1 = bf16[128,2,256]{2,1,0:T(2,128)(2,1)S(1)} async-done(((bf16[128,2,256]{2,1,0:T(2,128)(2,1)}), bf16[128,2,256]{2,1,0:T(2,128)(2,1)S(1)}, u32[]{:S(2)}, u32[]{:S(2)}) %all-to-all-start.1) | async-done | bytes 131104 | tf_op jit(solution)/shard_map/all_to_all | solution.py:85
  100.5 0.9 fusion.15
  101.6 102.8 %psum.37 = f32[256]{0:T(256)} all-reduce(f32[256]{0:T(256)S(1)} %get-tuple-element.22), channel_id=1, replica_groups=mesh['wide'=128,'narrow'=4] {'wide','narrow'}, use_global_device_ids=true, to_apply=%region_4.5 | all-reduce | flops 256 | bytes 2048 | tf_op jit(solution)/shard_map/psum | solution.py:112
  204.4 0.9 fusion.4
  205.3 351.8 %all-reduce.3.cloned.1.call-done = (f32[128,256]{0,1:T(8,128)}, f32[128,256]{1,0:T(8,128)}, f32[256,172]{0,1:T(8,128)}, f32[256,172]{0,1:T(8,128)}) async-done(((f32[128,256]{0,1:T(8,128)}, f32[128,256]{1,0:T(8,128)}, f32[256,172]{0,1:T(8,128)}, f32[256,172]{0,1:T(8,128)}), (f32[128,256]{0,1:T(8,128)}, f32[128,256]{1,0:T(8,128)}, f32[256,172]{0,1:T(8,128)}, ...) | async-done | bytes 614416 | tf_op jit(solution)/shard_map/psum | solution.py:112
  557.1 1.7 copy.31
  558.8 1.6 copy.48
  560.3 1.6 copy.49
  561.9 1.6 copy.50
  (57 shorter events, 12.7 us)
Async XLA Ops:
  7.2 28.8 %copy-start = (bf16[1,1,4,3,128,128]{5,4,3,2,1,0:T(8,128)(2,1)S(1)}, bf16[1,1,4,3,128,128]{5,4,3,2,1,0:T(8,128)(2,1)}, u32[]{:S(2)}) copy-start(bf16[1,1,4,3,128,128]{5,4,3,2,1,0:T(8,128)(2,1)} %param.15) | copy-start | bytes 1179652
  7.2 28.3 %copy-start.1 = (bf16[1,1,512,128]{3,2,1,0:T(8,128)(2,1)S(1)}, bf16[1,1,512,128]{3,2,1,0:T(8,128)(2,1)}, u32[]{:S(2)}) copy-start(bf16[1,1,512,128]{3,2,1,0:T(8,128)(2,1)} %param.11) | copy-start | bytes 393220
  7.2 28.3 %copy-start.6 = (bf16[128,256]{1,0:T(8,128)(2,1)S(1)}, bf16[128,256]{1,0:T(8,128)(2,1)}, u32[]{:S(2)}) copy-start(bf16[128,256]{1,0:T(8,128)(2,1)} %param.16) | copy-start | bytes 196612
  7.2 28.5 %copy-start.3 = (bf16[256,172]{0,1:T(8,128)(2,1)S(1)}, bf16[256,172]{0,1:T(8,128)(2,1)}, u32[]{:S(2)}) copy-start(bf16[256,172]{0,1:T(8,128)(2,1)} %param.20) | copy-start | bytes 264196
  11.5 35.2 %all-to-all-start = ((bf16[128,2,128]{2,1,0:T(2,128)(2,1)}), bf16[128,2,128]{2,1,0:T(2,128)(2,1)S(1)}, u32[]{:S(2)}, u32[]{:S(2)}) async-start(bf16[128,2,128]{2,1,0:T(2,128)(2,1)} %broadcast_select_fusion.1), calls=%async_computation | async-start | bytes 131072 | tf_op jit(solution)/shard_map/all_to_all | solution.py:69
  42.2 1.6 copy-start.2
  42.2 1.6 copy-start.4
  43.8 17.4 %copy-start.5 = (bf16[128,256]{1,0:T(8,128)(2,1)S(1)}, bf16[128,256]{1,0:T(8,128)(2,1)}, u32[]{:S(2)}) copy-start(bf16[128,256]{1,0:T(8,128)(2,1)} %param.17) | copy-start | bytes 196612
  43.8 17.4 %copy-start.7 = (f32[256]{0:T(256)S(1)}, f32[256]{0:T(256)}, u32[]{:S(2)}) copy-start(f32[256]{0:T(256)} %param.18) | copy-start | bytes 3076
  46.7 29.6 %all-to-all-start.2 = ((bf16[128,2,256]{2,1,0:T(2,128)(2,1)}), bf16[128,2,256]{2,1,0:T(2,128)(2,1)S(1)}, u32[]{:S(2)}, u32[]{:S(2)}) async-start(bf16[128,2,256]{2,1,0:T(2,128)(2,1)} %convert_element_type.58), calls=%async_computation.2 | async-start | bytes 262144 | tf_op jit(solution)/shard_map/all_to_all | solution.py:97
  76.2 23.2 %all-to-all-start.1 = ((bf16[128,2,256]{2,1,0:T(2,128)(2,1)}), bf16[128,2,256]{2,1,0:T(2,128)(2,1)S(1)}, u32[]{:S(2)}, u32[]{:S(2)}) async-start(bf16[128,2,256]{2,1,0:T(2,128)(2,1)} %broadcast_select_fusion), calls=%async_computation.1 | async-start | bytes 262144 | tf_op jit(solution)/shard_map/all_to_all | solution.py:85
  83.4 473.7 %all-reduce.3.cloned.1.call-start = ((), (), s32[]{:S(2)}) async-start(), calls=%async_computation.3 | async-start | bytes 1245184 | tf_op jit(solution)/shard_map/psum | solution.py:112
Sparse Core Ops, SparseCore 0:
  101.5 455.5 all-reduce.2
where the time goes:
time: 572 us; the launch traced here: 570 us
  waiting for transfers between devices  378 us (66%)
  blocking collectives  103 us (18%)
  starting transfers between devices  41.1 us (7%)
  local copies, waits for them, and re-layouts  19.8 us (3%)
  between operations  14.4 us (3%)
  matrix products  7.96 us (1%)
  other arithmetic  6.34 us (1%)
    psum x1, waiting for transfers between devices, shards(): lax.psum((first_self_weight_gradient, first_neighbour_weight_gradient, gr...  352 us
    psum x1, blocking collectives, shards(): lax.psum((first_self_weight_gradient, first_neighbour_weight_gradient, gr...  103 us
    all_to_all x1, starting transfers between devices, shards(): lax.all_to_all(outgoing(local_feat), 'wide', split_axis=0, concat_axis=0,...  20.4 us
    all_to_all x1, starting transfers between devices, shards(): lax.all_to_all(outbound.astype(jnp.bfloat16), 'wide', split_axis=0, conca...  13.5 us
    all_to_all x1, waiting for transfers between devices, shards(): lax.all_to_all(outbound.astype(jnp.bfloat16), 'wide', split_axis=0, conca...  11.9 us
    all_to_all x1, waiting for transfers between devices, shards(): lax.all_to_all(outgoing(hidden), 'wide', split_axis=0, concat_axis=0, til...  11.8 us
  transfers between devices with their start and end apart: 4, of which 4 were waited for; matrix products, arithmetic and copies ran while one was open for 4% of the time, Pallas kernels for 0%

commit v1 on v0

v1 whole, which is shorter than its diff:
```python
import jax
import jax.numpy as jnp
from jax import lax
from jax.experimental import pallas as pl
from jax.experimental.pallas import tpu as pltpu
from jax.sharding import Mesh, PartitionSpec as P

BF = jnp.bfloat16
F32 = jnp.float32
PLANE = ("x", "core", "y")
WIDE = ("z", "x", "core")
VM = pl.BlockSpec(memory_space=pltpu.VMEM)
SM = pl.BlockSpec(memory_space=pltpu.SMEM)
PARAMS = pltpu.CompilerParams(vmem_limit_bytes=32 * 1024 * 1024)


def dot(a, b):
    return jnp.dot(a, b, preferred_element_type=F32)


def dot_nt(a, b):
    return lax.dot_general(a, b, (((1,), (1,)), ((), ())), preferred_element_type=F32)


def split(values):
    upper = values.astype(BF)
    return upper, (values - upper.astype(F32)).astype(BF)


def before_kernel(index, rows, counts, feat, tiles, grad_t, send, pick, own_t, acc, padded):
    slot = lax.broadcasted_iota(jnp.int32, (2, 128), 0)
    wanted = jnp.where(slot < counts[...], rows[...], 512)
    by_slot = jnp.concatenate([wanted[0:1, :], wanted[1:2, :]], axis=1)
    i = lax.broadcasted_iota(jnp.int32, (256, 256), 0)
    j = lax.broadcasted_iota(jnp.int32, (256, 256), 1)
    place = jnp.where(j < 128, j * 2, (j - 128) * 2 + 1)
    perm = jnp.where(i == place, 1.0, 0.0).astype(BF)
    wide_rows = jnp.broadcast_to(by_slot, (128, 256))
    half = wide_rows // 2
    low = wide_rows - half * 2
    column = 2.0 * dot_nt(perm, half.astype(F32).astype(BF)) + dot_nt(perm, low.astype(F32).astype(BF))
    lane = lax.broadcasted_iota(jnp.int32, (256, 128), 1).astype(F32)
    for c in range(4):
        pick[:, c * 128 : (c + 1) * 128] = jnp.where(column == lane + 128.0 * c, 1.0, 0.0).astype(BF)
    send[:, 0:128] = dot(pick[...], feat[...]).astype(BF)
    padded[...] = jnp.zeros_like(padded)
    padded[0:172, :] = grad_t[...]
    acc[...] = jnp.zeros_like(acc)
    for b in range(4):
        part = padded[:, b * 128 : (b + 1) * 128]
        for k in range(3):
            e = index[b * 3 + k]
            acc[e] += dot(part, tiles[b * 3 + k])
    for b in range(4):
        own_t[:, b * 128 : (b + 1) * 128] = acc[b]
    for b in range(2):
        send[b * 128 : (b + 1) * 128, 128:384] = acc[4 + b].T.astype(BF)


def middle_kernel(
    index, recv, feat, tiles, pick, own_t, grad_t, w1s, w1n, bias, w2s_t, w2n_t,
    hidden, send, grads, ext, both, padded, wide_w,
):
    for b in range(4):
        ext[b] = feat[b * 128 : (b + 1) * 128, :]
    for b in range(2):
        ext[4 + b] = recv[b * 128 : (b + 1) * 128, 0:128]
    both[:, 0:128] = feat[...]
    for b in range(4):
        total = dot(tiles[b * 3], ext[index[b * 3]])
        total += dot(tiles[b * 3 + 1], ext[index[b * 3 + 1]])
        total += dot(tiles[b * 3 + 2], ext[index[b * 3 + 2]])
        both[b * 128 : (b + 1) * 128, 128:256] = total.astype(BF)
    pre = dot(both[:, 0:128], w1s[...]) + dot(both[:, 128:256], w1n[...]) + bias[...]
    hid = jnp.maximum(pre, 0.0).astype(BF)
    hidden[...] = hid
    send[...] = dot(pick[...], hid).astype(BF)
    padded[...] = jnp.zeros_like(padded)
    padded[0:172, :] = grad_t[...]
    wide_w[...] = jnp.zeros_like(wide_w)
    wide_w[0:172, :] = w2s_t[...]
    wide_w[256 : 256 + 172, :] = w2n_t[...]
    returned_t = recv[:, 128:384].astype(F32).T.astype(BF)
    back_t = own_t[...] + dot(returned_t, pick[...])
    upper_t, lower_t = split(back_t)
    upper, lower = split(back_t.T)
    grad = padded[...]
    grad_hidden = dot(grad.astype(F32).T.astype(BF), wide_w[0:256, :])
    grad_hidden += dot(upper, wide_w[256:512, :]) + dot(lower, wide_w[256:512, :])
    grad_pre = jnp.where(pre > 0, grad_hidden, 0.0).astype(BF)
    first = dot(both[...].astype(F32).T.astype(BF), grad_pre)
    bias_sum = jnp.sum(grad_pre.astype(F32), axis=0, keepdims=True)
    self2 = dot(grad, hid)
    neigh2 = dot(upper_t, hid) + dot(lower_t, hid)
    row = lax.broadcasted_iota(jnp.int32, (176, 256), 0)
    self2 = jnp.where(row == 172, bias_sum, self2[0:176, :])
    neigh2 = neigh2[0:176, :]
    for h in range(2):
        cols = slice(h * 128, (h + 1) * 128)
        base = h * 640
        grads[base : base + 256, :] = first[:, cols].astype(BF)
        grads[base + 256 : base + 432, :] = self2[:, cols].astype(BF)
        grads[base + 432 : base + 608, :] = neigh2[:, cols].astype(BF)
        grads[base + 608 : base + 640, :] = jnp.zeros((32, 128), BF)


def logits_kernel(index, recv, hidden, tiles, w2s_t, w2n_t, out_t, ext, agg):
    for b in range(4):
        ext[b] = hidden[b * 128 : (b + 1) * 128, :]
    for b in range(2):
        ext[4 + b] = recv[b * 128 : (b + 1) * 128, :]
    for b in range(4):
        total = dot(tiles[b * 3], ext[index[b * 3]])
        total += dot(tiles[b * 3 + 1], ext[index[b * 3 + 1]])
        total += dot(tiles[b * 3 + 2], ext[index[b * 3 + 2]])
        agg[b * 128 : (b + 1) * 128, :] = total.astype(BF)
    scores = dot_nt(w2s_t[...], hidden[...]) + dot_nt(w2n_t[...], agg[...])
    out_t[...] = scores.astype(BF)


def finish_kernel(total, self1, neigh1, bias, self2_t, neigh2_t):
    for h in range(2):
        cols = slice(h * 128, (h + 1) * 128)
        base = h * 640
        self1[:, cols] = total[base : base + 128, :].astype(F32)
        neigh1[:, cols] = total[base + 128 : base + 256, :].astype(F32)
        self2 = total[base + 256 : base + 432, :].astype(F32)
        self2_t[:, cols] = self2[0:172, :]
        bias[:, cols] = self2[172:173, :]
        neigh2_t[:, cols] = total[base + 432 : base + 608, :].astype(F32)[0:172, :]


def shape(dims, dtype):
    return jax.ShapeDtypeStruct(dims, dtype)


def before(index, rows, counts, feat, tiles, grad_t):
    return pl.pallas_call(
        before_kernel,
        out_shape=(shape((256, 384), BF), shape((256, 512), BF), shape((256, 512), F32)),
        in_specs=[SM, VM, VM, VM, VM, VM],
        out_specs=(VM, VM, VM),
        scratch_shapes=[pltpu.VMEM((6, 256, 128), F32), pltpu.VMEM((256, 512), BF)],
        compiler_params=PARAMS,
    )(index, rows, counts, feat, tiles, grad_t)


def middle(index, recv, feat, tiles, pick, own_t, grad_t, w1s, w1n, bias, w2s_t, w2n_t):
    return pl.pallas_call(
        middle_kernel,
        out_shape=(shape((512, 256), BF), shape((256, 256), BF), shape((1280, 128), BF)),
        in_specs=[SM] + [VM] * 11,
        out_specs=(VM, VM, VM),
        scratch_shapes=[
            pltpu.VMEM((6, 128, 128), BF),
            pltpu.VMEM((512, 256), BF),
            pltpu.VMEM((256, 512), BF),
            pltpu.VMEM((512, 256), BF),
        ],
        compiler_params=PARAMS,
    )(index, recv, feat, tiles, pick, own_t, grad_t, w1s, w1n, bias, w2s_t, w2n_t)


def scores(index, recv, hidden, tiles, w2s_t, w2n_t):
    return pl.pallas_call(
        logits_kernel,
        out_shape=shape((172, 512), BF),
        in_specs=[SM] + [VM] * 5,
        out_specs=VM,
        scratch_shapes=[pltpu.VMEM((6, 128, 256), BF), pltpu.VMEM((512, 256), BF)],
        compiler_params=PARAMS,
    )(index, recv, hidden, tiles, w2s_t, w2n_t)


def finish(total):
    return pl.pallas_call(
        finish_kernel,
        out_shape=(
            shape((128, 256), F32),
            shape((128, 256), F32),
            shape((1, 256), F32),
            shape((172, 256), F32),
            shape((172, 256), F32),
        ),
        in_specs=[VM],
        out_specs=(VM,) * 5,
        compiler_params=PARAMS,
    )(total)


def exchange(values, axes):
    return lax.all_to_all(values, axes, split_axis=0, concat_axis=0, tiled=True)


def shards(
    features,
    send_rows,
    send_counts,
    tile_index,
    tile_weight,
    first_layer_self_weight,
    first_layer_neighbour_weight,
    layer1_bias,
    layer2_self,
    layer2_neigh,
    grad_logits,
):
    feat = features.reshape(512, 128)
    rows = jnp.swapaxes(send_rows.reshape(128, 2), 0, 1)
    counts = send_counts.reshape(1, 128)
    index = tile_index.reshape(12)
    tiles = tile_weight.reshape(12, 128, 128)
    grad_t = jnp.swapaxes(grad_logits.reshape(512, 172), 0, 1)
    w2s_t = jnp.swapaxes(layer2_self, 0, 1)
    w2n_t = jnp.swapaxes(layer2_neigh, 0, 1)
    bias = layer1_bias.reshape(1, 256)

    send1, pick, own_t = before(index, rows, counts, feat, tiles, grad_t)
    recv1 = exchange(send1.reshape(128, 2, 384), WIDE).reshape(256, 384)
    hidden, send2, grads = middle(
        index, recv1, feat, tiles, pick, own_t, grad_t,
        first_layer_self_weight, first_layer_neighbour_weight, bias, w2s_t, w2n_t,
    )

    parts = exchange(grads.reshape(32, 40, 128), PLANE)
    recv2 = exchange(send2.reshape(128, 2, 256), WIDE).reshape(256, 256)
    chunk = jnp.sum(parts.astype(F32), axis=0).astype(BF)
    layers = exchange(jnp.broadcast_to(chunk[None], (16, 40, 128)), "z")
    chunk = jnp.sum(layers.astype(F32), axis=0).astype(BF)
    total = exchange(jnp.broadcast_to(chunk[None], (32, 40, 128)), PLANE)
    logits_t = scores(index, recv2, hidden, tiles, w2s_t, w2n_t)
    self1, neigh1, bias1, self2_t, neigh2_t = finish(total.reshape(1280, 128))
    logits = jnp.swapaxes(logits_t, 0, 1).reshape(1, 1, 512, 172)
    return (
        logits,
        self1,
        neigh1,
        bias1.reshape(256),
        jnp.swapaxes(self2_t, 0, 1),
        jnp.swapaxes(neigh2_t, 0, 1),
    )


def solution(mesh):
    fine = Mesh(mesh.devices.reshape(16, 4, 2, 4), ("z", "x", "core", "y"))
    return jax.shard_map(
        shards,
        mesh=fine,
        in_specs=(
            P(WIDE, "y", None, None),
            P(WIDE, "y", None, None),
            P(WIDE, "y", None),
            P(WIDE, "y", None, None),
            P(WIDE, "y", None, None, None, None),
            P(),
            P(),
            P(),
            P(),
            P(),
            P(WIDE, "y", None, None),
        ),
        out_specs=(P(WIDE, "y", None, None), P(), P(), P(), P(), P()),
        check_vma=False,
    )
```

time: 572 us -> 126 us (0.22)
  waiting for transfers between devices: 378 us -> 35.1 us
  blocking collectives: 103 us -> 55.8 us
  starting transfers between devices: 41.1 us -> 19.4 us
  between operations: 14.4 us -> 0.78 us
  local copies, waits for them, and re-layouts: 19.8 us -> 7.67 us
  matrix products: 7.96 us -> 0 us
  Pallas kernels: 0 us -> 6.58 us
  other arithmetic: 6.34 us -> 0.09 us
    psum x1 -> x0, waiting for transfers between devices: 352 us -> none  [shards(): lax.psum((first_self_weight_gradient, first_neighbour_weight_gradient, gr...]
    psum x1 -> x0, blocking collectives: 103 us -> none  [shards(): lax.psum((first_self_weight_gradient, first_neighbour_weight_gradient, gr...]
    all_to_all x0 -> x2, blocking collectives: none -> 55.8 us  [exchange(): return lax.all_to_all(values, axes, split_axis=0, concat_axis=0, tiled=True)]
    all_to_all x3, starting transfers between devices: 41 us -> 19.4 us  [exchange(): return lax.all_to_all(values, axes, split_axis=0, concat_axis=0, tiled=True)]
    all_to_all x3, waiting for transfers between devices: 26.3 us -> 35.1 us  [exchange(): return lax.all_to_all(values, axes, split_axis=0, concat_axis=0, tiled=True)]
    dot_general x15 -> x0, matrix products: 7.96 us -> none  [the longest x1 0.92 us: shards(): jnp.dot(local_feat.T, grad_pre, preferred_element_type=jnp.float32)]
    pallas_call x0 -> x4, Pallas kernels: none -> 6.58 us  [the longest x1 2.56 us: middle(): pl.pallas_call(middle_kernel, out_shape=(shape((512, 256), BF), shape((25...]
  transfers between devices with their start and end apart: 4 -> 3, of which waited for: 4 -> 3; matrix products, arithmetic and copies ran while one was open for 4% -> 1% of each run, Pallas kernels for 0% -> 1%
where the time goes in v1:
time: 126 us; the launch traced here: 125 us
  blocking collectives  55.8 us (44%)
  waiting for transfers between devices  35.1 us (28%)
  starting transfers between devices  19.4 us (15%)
  local copies, waits for them, and re-layouts  7.67 us (6%)
  Pallas kernels  6.58 us (5%)
    all_to_all x2, blocking collectives, exchange(): return lax.all_to_all(values, axes, split_axis=0, concat_axis=0, tiled=True)  55.8 us
    all_to_all x3, waiting for transfers between devices, exchange(): return lax.all_to_all(values, axes, split_axis=0, concat_axis=0, tiled=True)  35.1 us
    all_to_all x3, starting transfers between devices, exchange(): return lax.all_to_all(values, axes, split_axis=0, concat_axis=0, tiled=True)  19.4 us
    unnamed x27, local copies, waits for them, and re-layouts  5.21 us
    pallas_call x1, Pallas kernels, middle(): pl.pallas_call(middle_kernel, out_shape=(shape((512, 256), BF), shape((25...  2.56 us
  transfers between devices with their start and end apart: 3, of which 3 were waited for; matrix products, arithmetic and copies ran while one was open for 1% of the time, Pallas kernels for 1%

profile of v1, /device:TPU:1, one launch (start us, length us, event | category | flops | bytes accessed | tf_op | source)
XLA Modules:
  0.0 125.4 jit_solution(8440439881650892536)
XLA Ops:
  0.6 0.8 copy.19
  1.4 0.1 reshape.59.index
  1.5 0.7 copy-done.10
  2.2 1.0 copy-done
  3.2 0.9 copy-done.2
  4.1 0.9 copy-done.4
  5.0 1.3 %shard_map.154 = (bf16[256,384]{1,0:T(8,128)(2,1)S(1)}, bf16[256,512]{1,0:T(8,128)(2,1)S(1)}, f32[256,512]{1,0:T(8,128)S(1)}) custom-call(s32[12]{0:T(128)S(1)} %reshape.59.index, s32[2,128]{1,0:T(2,128)S(1)} %bitcast.33, s32[1,128]{1,0:T(1,128)S(1)} %bitcast.35, bf16[512,128]{1,0:T(8,128)(2,1)S(1)} %bitcast.26, bf16[12,128,128]{2,1,0:T(8,128)(2,1)S(1)} %bitcast.20, ...), custom_call_target="tpu_custom_call" | custom-call | tf_op jit(solution)/shard_map/pallas_call | solution.py:138
  6.3 0.1 reshape.65
  6.4 38.4 %all_to_all.25 = bf16[128,2,384]{2,1,0:T(2,128)(2,1)S(1)} all-to-all(bf16[128,2,384]{2,1,0:T(2,128)(2,1)S(1)} %reshape.65), channel_id=1, replica_groups=mesh['z'=16,'x'=4,'core'=2,'y'=4] {'z','x','core'}, dimensions={0} | all-to-all | bytes 393216 | tf_op jit(solution)/shard_map/all_to_all | solution.py:192
  44.8 0.1 reshape.66.recv
  44.9 0.8 copy-done.3
  45.8 2.6 %shard_map.155 = (bf16[512,256]{1,0:T(8,128)(2,1)S(1)}, bf16[256,256]{1,0:T(8,128)(2,1)S(1)}, bf16[1280,128]{1,0:T(8,128)(2,1)S(1)}) custom-call(s32[12]{0:T(128)S(1)} %reshape.59.index, bf16[256,384]{1,0:T(8,128)(2,1)S(1)} %reshape.66.recv, bf16[512,128]{1,0:T(8,128)(2,1)S(1)} %bitcast.27, bf16[12,128,128]{2,1,0:T(8,128)(2,1)S(1)} %bitcast.21, ...), custom_call_target="tpu_custom_call" | custom-call | tf_op jit(solution)/shard_map/pallas_call | solution.py:149
  48.4 17.4 %all_to_all.26 = bf16[32,40,128]{2,1,0:T(8,128)(2,1)S(1)} all-to-all(bf16[32,40,128]{2,1,0:T(8,128)(2,1)S(1)} %bitcast.32), channel_id=1, replica_groups=mesh['z'=16,'x'=4,'core'=2,'y'=4] {'x','core','y'}, dimensions={0} | all-to-all | bytes 655360 | tf_op jit(solution)/shard_map/all_to_all | solution.py:192
  65.9 0.7 broadcast_in_dim.4
  66.6 3.5 %all-to-all-start.3 = ((bf16[16,40,128]{2,1,0:T(8,128)(2,1)}), bf16[16,40,128]{2,1,0:T(8,128)(2,1)S(1)}, u32[]{:S(2)}, u32[]{:S(2)}) async-start(bf16[16,40,128]{2,1,0:T(8,128)(2,1)} %broadcast_in_dim.4), calls=%async_computation.3 | async-start | bytes 327680 | tf_op jit(solution)/shard_map/all_to_all | solution.py:192
  70.1 0.7 reshape.68
  70.8 11.5 %all-to-all-done.3 = bf16[16,40,128]{2,1,0:T(8,128)(2,1)S(1)} async-done(((bf16[16,40,128]{2,1,0:T(8,128)(2,1)}), bf16[16,40,128]{2,1,0:T(8,128)(2,1)S(1)}, u32[]{:S(2)}, u32[]{:S(2)}) %all-to-all-start.3) | async-done | bytes 163872 | tf_op jit(solution)/shard_map/all_to_all | solution.py:192
  82.3 10.6 %all-to-all-start.1 = ((bf16[128,2,256]{2,1,0:T(2,128)(2,1)}), bf16[128,2,256]{2,1,0:T(2,128)(2,1)S(1)}, u32[]{:S(2)}, u32[]{:S(2)}) async-start(bf16[128,2,256]{2,1,0:T(2,128)(2,1)} %reshape.68), calls=%async_computation.1 | async-start | bytes 262144 | tf_op jit(solution)/shard_map/all_to_all | solution.py:192
  93.0 16.0 %all-to-all-done.1 = bf16[128,2,256]{2,1,0:T(2,128)(2,1)S(1)} async-done(((bf16[128,2,256]{2,1,0:T(2,128)(2,1)}), bf16[128,2,256]{2,1,0:T(2,128)(2,1)S(1)}, u32[]{:S(2)}, u32[]{:S(2)}) %all-to-all-start.1) | async-done | bytes 131104 | tf_op jit(solution)/shard_map/all_to_all | solution.py:192
  109.1 0.8 broadcast_in_dim.5
  109.8 5.3 %all-to-all-start.4 = ((bf16[32,40,128]{2,1,0:T(8,128)(2,1)}), bf16[32,40,128]{2,1,0:T(8,128)(2,1)S(1)}, u32[]{:S(2)}, u32[]{:S(2)}) async-start(bf16[32,40,128]{2,1,0:T(8,128)(2,1)} %broadcast_in_dim.5), calls=%async_computation.4 | async-start | bytes 655360 | tf_op jit(solution)/shard_map/all_to_all | solution.py:192
  115.2 1.9 %shard_map.156 = bf16[172,512]{1,0:T(8,128)(2,1)} custom-call(s32[12]{0:T(128)S(1)} %reshape.59.index, bf16[256,256]{1,0:T(8,128)(2,1)S(1)} %reshape.69.recv, bf16[512,256]{1,0:T(8,128)(2,1)S(1)} %get-tuple-element.21.hidden, bf16[12,128,128]{2,1,0:T(8,128)(2,1)S(1)} %bitcast.22, bf16[172,256]{1,0:T(8,128)(2,1)S(1)} %bitcast.29, bf16[172,256]{1,0:T(8,128)(2,1)S(1)} %bitcast.31), custom_call_target="tpu_custom_call" | custom-call | tf_op jit(solution)/shard_map/pallas_call | solution.py:165
  117.0 7.5 %all-to-all-done.4 = bf16[32,40,128]{2,1,0:T(8,128)(2,1)S(1)} async-done(((bf16[32,40,128]{2,1,0:T(8,128)(2,1)}), bf16[32,40,128]{2,1,0:T(8,128)(2,1)S(1)}, u32[]{:S(2)}, u32[]{:S(2)}) %all-to-all-start.4) | async-done | bytes 327712 | tf_op jit(solution)/shard_map/all_to_all | solution.py:192
  124.6 0.8 shard_map.157
  (24 shorter events, 0.3 us)
Async XLA Ops:
  1.5 0.7 copy-start.10
  1.5 0.7 copy-start.12
  2.2 1.0 copy-start
  3.2 0.9 copy-start.2
  4.1 0.9 copy-start.4
  6.3 38.6 %copy-start.7 = (bf16[256,172]{0,1:T(8,128)(2,1)S(1)}, bf16[256,172]{0,1:T(8,128)(2,1)}, u32[]{:S(2)}) copy-start(bf16[256,172]{0,1:T(8,128)(2,1)} %param.20) | copy-start | bytes 264196
  6.3 38.6 %copy-start.8 = (bf16[128,256]{1,0:T(8,128)(2,1)S(1)}, bf16[128,256]{1,0:T(8,128)(2,1)}, u32[]{:S(2)}) copy-start(bf16[128,256]{1,0:T(8,128)(2,1)} %w1s.1) | copy-start | bytes 196612
  6.3 38.6 %copy-start.9 = (bf16[128,256]{1,0:T(8,128)(2,1)S(1)}, bf16[128,256]{1,0:T(8,128)(2,1)}, u32[]{:S(2)}) copy-start(bf16[128,256]{1,0:T(8,128)(2,1)} %w1n.1) | copy-start | bytes 196612
  6.4 38.5 %copy-start.1 = (bf16[1,1,4,3,128,128]{5,4,3,2,1,0:T(8,128)(2,1)S(1)}, bf16[1,1,4,3,128,128]{5,4,3,2,1,0:T(8,128)(2,1)}, u32[]{:S(2)}) copy-start(bf16[1,1,4,3,128,128]{5,4,3,2,1,0:T(8,128)(2,1)} %param.15) | copy-start | bytes 1179652
  44.8 0.9 copy-start.3
  44.8 1.0 copy-start.5
  44.8 1.0 copy-start.6
  44.9 1.0 copy-start.11
  66.6 15.8 %all-to-all-start.3 = ((bf16[16,40,128]{2,1,0:T(8,128)(2,1)}), bf16[16,40,128]{2,1,0:T(8,128)(2,1)S(1)}, u32[]{:S(2)}, u32[]{:S(2)}) async-start(bf16[16,40,128]{2,1,0:T(8,128)(2,1)} %broadcast_in_dim.4), calls=%async_computation.3 | async-start | bytes 327680 | tf_op jit(solution)/shard_map/all_to_all | solution.py:192
  82.3 26.7 %all-to-all-start.1 = ((bf16[128,2,256]{2,1,0:T(2,128)(2,1)}), bf16[128,2,256]{2,1,0:T(2,128)(2,1)S(1)}, u32[]{:S(2)}, u32[]{:S(2)}) async-start(bf16[128,2,256]{2,1,0:T(2,128)(2,1)} %reshape.68), calls=%async_computation.1 | async-start | bytes 262144 | tf_op jit(solution)/shard_map/all_to_all | solution.py:192
  109.8 14.7 %all-to-all-start.4 = ((bf16[32,40,128]{2,1,0:T(8,128)(2,1)}), bf16[32,40,128]{2,1,0:T(8,128)(2,1)S(1)}, u32[]{:S(2)}, u32[]{:S(2)}) async-start(bf16[32,40,128]{2,1,0:T(8,128)(2,1)} %broadcast_in_dim.5), calls=%async_computation.4 | async-start | bytes 655360 | tf_op jit(solution)/shard_map/all_to_all | solution.py:192

commit v2 on v1

--- a/solution.py
+++ b/solution.py
@@ -27,14 +27,26 @@
     return upper, (values - upper.astype(F32)).astype(BF)
 
 
-def before_kernel(index, rows, counts, feat, tiles, grad_t, send, pick, own_t, acc, padded):
-    slot = lax.broadcasted_iota(jnp.int32, (2, 128), 0)
-    wanted = jnp.where(slot < counts[...], rows[...], 512)
-    by_slot = jnp.concatenate([wanted[0:1, :], wanted[1:2, :]], axis=1)
+def before_kernel(*refs):
+    rows_in, counts_in = refs[0:2]
+    send, pick, own_t = refs[11:14]
+    feat, grad_t, tiles = refs[14:17]
+    rows, counts, index, acc, padded, sems = refs[23:29]
+    pairs = [(rows_in, rows), (counts_in, counts)] + list(zip(refs[2:11], refs[14:23])) + [(refs[10], index)]
+    copies = [pltpu.make_async_copy(a, b, sems.at[i]) for i, (a, b) in enumerate(pairs)]
+    for copy in copies:
+        copy.start()
+    acc[...] = jnp.zeros_like(acc)
+    padded[...] = jnp.zeros_like(padded)
     i = lax.broadcasted_iota(jnp.int32, (256, 256), 0)
     j = lax.broadcasted_iota(jnp.int32, (256, 256), 1)
     place = jnp.where(j < 128, j * 2, (j - 128) * 2 + 1)
     perm = jnp.where(i == place, 1.0, 0.0).astype(BF)
+    copies[0].wait()
+    copies[1].wait()
+    slot = lax.broadcasted_iota(jnp.int32, (2, 128), 0)
+    wanted = jnp.where(slot < counts[...], rows[...], 512)
+    by_slot = jnp.concatenate([wanted[0:1, :], wanted[1:2, :]], axis=1)
     wide_rows = jnp.broadcast_to(by_slot, (128, 256))
     half = wide_rows // 2
     low = wide_rows - half * 2
@@ -42,24 +54,35 @@
     lane = lax.broadcasted_iota(jnp.int32, (256, 128), 1).astype(F32)
     for c in range(4):
         pick[:, c * 128 : (c + 1) * 128] = jnp.where(column == lane + 128.0 * c, 1.0, 0.0).astype(BF)
+    copies[2].wait()
     send[:, 0:128] = dot(pick[...], feat[...]).astype(BF)
-    padded[...] = jnp.zeros_like(padded)
+    copies[3].wait()
     padded[0:172, :] = grad_t[...]
-    acc[...] = jnp.zeros_like(acc)
+    copies[4].wait()
+    copies[11].wait()
     for b in range(4):
         part = padded[:, b * 128 : (b + 1) * 128]
         for k in range(3):
-            e = index[b * 3 + k]
+            e = index[k, 0, b]
             acc[e] += dot(part, tiles[b * 3 + k])
     for b in range(4):
         own_t[:, b * 128 : (b + 1) * 128] = acc[b]
     for b in range(2):
         send[b * 128 : (b + 1) * 128, 128:384] = acc[4 + b].T.astype(BF)
+    for copy in copies[5:11]:
+        copy.wait()
+
+
+def gather_tiles(index, tiles, ext, b):
+    total = dot(tiles[b * 3], ext[index[0, 0, b]])
+    total += dot(tiles[b * 3 + 1], ext[index[1, 0, b]])
+    total += dot(tiles[b * 3 + 2], ext[index[2, 0, b]])
+    return total.astype(BF)
 
 
 def middle_kernel(
     index, recv, feat, tiles, pick, own_t, grad_t, w1s, w1n, bias, w2s_t, w2n_t,
-    hidden, send, grads, ext, both, padded, wide_w,
+    hidden, out, ext, both, padded, wide_w, grads,
 ):
     for b in range(4):
         ext[b] = feat[b * 128 : (b + 1) * 128, :]
@@ -67,14 +90,18 @@
         ext[4 + b] = recv[b * 128 : (b + 1) * 128, 0:128]
     both[:, 0:128] = feat[...]
     for b in range(4):
-        total = dot(tiles[b * 3], ext[index[b * 3]])
-        total += dot(tiles[b * 3 + 1], ext[index[b * 3 + 1]])
-        total += dot(tiles[b * 3 + 2], ext[index[b * 3 + 2]])
-        both[b * 128 : (b + 1) * 128, 128:256] = total.astype(BF)
+        both[b * 128 : (b + 1) * 128, 128:256] = gather_tiles(index, tiles, ext, b)
     pre = dot(both[:, 0:128], w1s[...]) + dot(both[:, 128:256], w1n[...]) + bias[...]
     hid = jnp.maximum(pre, 0.0).astype(BF)
     hidden[...] = hid
-    send[...] = dot(pick[...], hid).astype(BF)
+    i = lax.broadcasted_iota(jnp.int32, (256, 256), 0)
+    j = lax.broadcasted_iota(jnp.int32, (256, 256), 1)
+    place = ((i // 2) % 16) * 16 + (i // 32) * 2 + i % 2
+    perm = jnp.where(j == place, 1.0, 0.0).astype(BF)
+    picked = dot(perm, dot(pick[...], hid).astype(BF)).astype(BF)
+    for p in range(8):
+        out[p, 160:192, :] = picked[p * 32 : (p + 1) * 32, 0:128]
+        out[p, 192:224, :] = picked[p * 32 : (p + 1) * 32, 128:256]
     padded[...] = jnp.zeros_like(padded)
     padded[0:172, :] = grad_t[...]
     wide_w[...] = jnp.zeros_like(wide_w)
@@ -102,18 +129,55 @@
         grads[base + 256 : base + 432, :] = self2[:, cols].astype(BF)
         grads[base + 432 : base + 608, :] = neigh2[:, cols].astype(BF)
         grads[base + 608 : base + 640, :] = jnp.zeros((32, 128), BF)
+    for p in range(8):
+        out[p, 0:160, :] = grads[p * 160 : (p + 1) * 160, :]
+
+
+def plane_kernel(parts, chunk, hidden):
+    total = parts[0, 0:160, :].astype(F32)
+    for p in range(1, 8):
+        total += parts[p, 0:160, :].astype(F32)
+    total = total.astype(BF)
+    for q in range(4):
+        chunk[q] = total[q * 40 : (q + 1) * 40, :]
+    i = lax.broadcasted_iota(jnp.int32, (256, 256), 0)
+    j = lax.broadcasted_iota(jnp.int32, (256, 256), 1)
+    place = ((i // 2) % 8) * 32 + (i // 16) * 2 + i % 2
+    perm = jnp.where(j == place, 1.0, 0.0).astype(BF)
+    for h in range(2):
+        rows = jnp.concatenate([parts[p, 160 + h * 32 : 192 + h * 32, :] for p in range(8)], axis=0)
+        hidden[:, h * 128 : (h + 1) * 128] = dot(perm, rows).astype(BF)
+
+
+def column_kernel(parts, hidden, out):
+    total = parts[0].astype(F32)
+    for p in range(1, 4):
+        total += parts[p].astype(F32)
+    total = total.astype(BF)
+    for z in range(16):
+        out[z, 0:16, :] = hidden[z * 16 : (z + 1) * 16, 0:128]
+        out[z, 16:32, :] = hidden[z * 16 : (z + 1) * 16, 128:256]
+        out[z, 32:72, :] = total
+
+
+def layer_kernel(parts, out):
+    total = parts[0, 32:72, :].astype(F32)
+    for p in range(1, 16):
+        total += parts[p, 32:72, :].astype(F32)
+    total = total.astype(BF)
+    for p in range(32):
+        out[p] = total
 
 
 def logits_kernel(index, recv, hidden, tiles, w2s_t, w2n_t, out_t, ext, agg):
     for b in range(4):
         ext[b] = hidden[b * 128 : (b + 1) * 128, :]
-    for b in range(2):
-        ext[4 + b] = recv[b * 128 : (b + 1) * 128, :]
-    for b in range(4):
-        total = dot(tiles[b * 3], ext[index[b * 3]])
-        total += dot(tiles[b * 3 + 1], ext[index[b * 3 + 1]])
-        total += dot(tiles[b * 3 + 2], ext[index[b * 3 + 2]])
-        agg[b * 128 : (b + 1) * 128, :] = total.astype(BF)
+    for z in range(16):
+        rows = slice((z % 8) * 16, (z % 8) * 16 + 16)
+        ext[4 + z // 8, rows, 0:128] = recv[z, 0:16, :]
+        ext[4 + z // 8, rows, 128:256] = recv[z, 16:32, :]
+    for b in range(4):
+        agg[b * 128 : (b + 1) * 128, :] = gather_tiles(index, tiles, ext, b)
     scores = dot_nt(w2s_t[...], hidden[...]) + dot_nt(w2n_t[...], agg[...])
     out_t[...] = scores.astype(BF)
 
@@ -134,28 +198,38 @@
     return jax.ShapeDtypeStruct(dims, dtype)
 
 
-def before(index, rows, counts, feat, tiles, grad_t):
+def before(rows, counts, *kept):
+    here = [pltpu.with_memory_space_constraint(value, pltpu.HBM) for value in (rows, counts) + kept]
     return pl.pallas_call(
         before_kernel,
-        out_shape=(shape((256, 384), BF), shape((256, 512), BF), shape((256, 512), F32)),
-        in_specs=[SM, VM, VM, VM, VM, VM],
-        out_specs=(VM, VM, VM),
-        scratch_shapes=[pltpu.VMEM((6, 256, 128), F32), pltpu.VMEM((256, 512), BF)],
-        compiler_params=PARAMS,
-    )(index, rows, counts, feat, tiles, grad_t)
+        out_shape=(shape((256, 384), BF), shape((256, 512), BF), shape((256, 512), F32))
+        + tuple(shape(value.shape, value.dtype) for value in kept),
+        in_specs=[pl.BlockSpec(memory_space=pltpu.HBM)] * 11,
+        out_specs=(VM,) * 12,
+        scratch_shapes=[
+            pltpu.VMEM((2, 128), jnp.int32),
+            pltpu.VMEM((1, 128), jnp.int32),
+            pltpu.SMEM((3, 1, 4), jnp.int32),
+            pltpu.VMEM((6, 256, 128), F32),
+            pltpu.VMEM((256, 512), BF),
+            pltpu.SemaphoreType.DMA((12,)),
+        ],
+        compiler_params=PARAMS,
+    )(*here)
 
 
 def middle(index, recv, feat, tiles, pick, own_t, grad_t, w1s, w1n, bias, w2s_t, w2n_t):
     return pl.pallas_call(
         middle_kernel,
-        out_shape=(shape((512, 256), BF), shape((256, 256), BF), shape((1280, 128), BF)),
+        out_shape=(shape((512, 256), BF), shape((8, 224, 128), BF)),
         in_specs=[SM] + [VM] * 11,
-        out_specs=(VM, VM, VM),
+        out_specs=(VM, VM),
         scratch_shapes=[
             pltpu.VMEM((6, 128, 128), BF),
             pltpu.VMEM((512, 256), BF),
             pltpu.VMEM((256, 512), BF),
             pltpu.VMEM((512, 256), BF),
+            pltpu.VMEM((1280, 128), BF),
         ],
         compiler_params=PARAMS,
     )(index, recv, feat, tiles, pick, own_t, grad_t, w1s, w1n, bias, w2s_t, w2n_t)
@@ -170,6 +244,36 @@
         scratch_shapes=[pltpu.VMEM((6, 128, 256), BF), pltpu.VMEM((512, 256), BF)],
         compiler_params=PARAMS,
     )(index, recv, hidden, tiles, w2s_t, w2n_t)
+
+
+def after_plane(parts):
+    return pl.pallas_call(
+        plane_kernel,
+        out_shape=(shape((4, 40, 128), BF), shape((256, 256), BF)),
+        in_specs=[VM],
+        out_specs=(VM, VM),
+        compiler_params=PARAMS,
+    )(parts)
+
+
+def after_column(parts, hidden):
+    return pl.pallas_call(
+        column_kernel,
+        out_shape=shape((16, 72, 128), BF),
+        in_specs=[VM, VM],
+        out_specs=VM,
+        compiler_params=PARAMS,
+    )(parts, hidden)
+
+
+def after_layers(parts):
+    return pl.pallas_call(
+        layer_kernel,
+        out_shape=shape((32, 40, 128), BF),
+        in_specs=[VM],
+        out_specs=VM,
+        compiler_params=PARAMS,
+    )(parts)
 
 
 def finish(total):
@@ -208,26 +312,25 @@
     feat = features.reshape(512, 128)
     rows = jnp.swapaxes(send_rows.reshape(128, 2), 0, 1)
     counts = send_counts.reshape(1, 128)
-    index = tile_index.reshape(12)
+    index = jnp.transpose(tile_index, (0, 3, 1, 2)).reshape(3, 1, 4)
     tiles = tile_weight.reshape(12, 128, 128)
     grad_t = jnp.swapaxes(grad_logits.reshape(512, 172), 0, 1)
     w2s_t = jnp.swapaxes(layer2_self, 0, 1)
     w2n_t = jnp.swapaxes(layer2_neigh, 0, 1)
     bias = layer1_bias.reshape(1, 256)
 
-    send1, pick, own_t = before(index, rows, counts, feat, tiles, grad_t)
+    send1, pick, own_t, feat, grad_t, tiles, w1s, w1n, bias, w2s_t, w2n_t, index = before(
+        rows, counts, feat, grad_t, tiles,
+        first_layer_self_weight, first_layer_neighbour_weight, bias, w2s_t, w2n_t, index,
+    )
     recv1 = exchange(send1.reshape(128, 2, 384), WIDE).reshape(256, 384)
-    hidden, send2, grads = middle(
+    hidden, parts = middle(
         index, recv1, feat, tiles, pick, own_t, grad_t,
-        first_layer_self_weight, first_layer_neighbour_weight, bias, w2s_t, w2n_t,
+        w1s, w1n, bias, w2s_t, w2n_t,
     )
-
-    parts = exchange(grads.reshape(32, 40, 128), PLANE)
-    recv2 = exchange(send2.reshape(128, 2, 256), WIDE).reshape(256, 256)
-    chunk = jnp.sum(parts.astype(F32), axis=0).astype(BF)
-    layers = exchange(jnp.broadcast_to(chunk[None], (16, 40, 128)), "z")
-    chunk = jnp.sum(layers.astype(F32), axis=0).astype(BF)
-    total = exchange(jnp.broadcast_to(chunk[None], (32, 40, 128)), PLANE)
+    chunk, passing = after_plane(exchange(parts, ("x", "core")))
+    recv2 = exchange(after_column(exchange(chunk, "y"), passing), "z")
+    total = exchange(after_layers(recv2), PLANE)
     logits_t = scores(index, recv2, hidden, tiles, w2s_t, w2n_t)
     self1, neigh1, bias1, self2_t, neigh2_t = finish(total.reshape(1280, 128))
     logits = jnp.swapaxes(logits_t, 0, 1).reshape(1, 1, 512, 172)

time: 126 us -> 105 us (0.83)
  waiting for transfers between devices: 35.1 us -> 7.65 us
  blocking collectives: 55.8 us -> 76.4 us
  starting transfers between devices: 19.4 us -> 11.2 us
  local copies, waits for them, and re-layouts: 7.67 us -> 0.15 us
  Pallas kernels: 6.58 us -> 8.35 us
    all_to_all x3 -> x1, waiting for transfers between devices: 35.1 us -> 7.65 us  [exchange(): return lax.all_to_all(values, axes, split_axis=0, concat_axis=0, tiled=True)]
    all_to_all x2 -> x4, blocking collectives: 55.8 us -> 76.4 us  [exchange(): return lax.all_to_all(values, axes, split_axis=0, concat_axis=0, tiled=True)]
    all_to_all x3 -> x1, starting transfers between devices: 19.4 us -> 11.2 us  [exchange(): return lax.all_to_all(values, axes, split_axis=0, concat_axis=0, tiled=True)]
    unnamed x27 -> x0, local copies, waits for them, and re-layouts: 5.21 us -> none
    broadcast_in_dim x2 -> x0, local copies, waits for them, and re-layouts: 1.46 us -> none  [the longest x1 0.77 us: shards(): total = exchange(jnp.broadcast_to(chunk[None], (32, 40, 128)), PLANE)]
    pallas_call x1 -> x4, Pallas kernels: 2.56 us -> 3.79 us  [the longest x1 2.74 us: middle(): pl.pallas_call(middle_kernel, out_shape=(shape((512, 256), BF), shape((8,...]
  transfers between devices with their start and end apart: 3 -> 1, of which waited for: 3 -> 1; matrix products, arithmetic and copies ran while one was open for 1% -> 0% of each run, Pallas kernels for 1% -> 2%
where the time goes in v2:
time: 105 us; the launch traced here: 104 us
  blocking collectives  76.4 us (73%)
  starting transfers between devices  11.2 us (11%)
  Pallas kernels  8.35 us (8%)
  waiting for transfers between devices  7.65 us (7%)
    all_to_all x4, blocking collectives, exchange(): return lax.all_to_all(values, axes, split_axis=0, concat_axis=0, tiled=True)  76.4 us
    all_to_all x1, starting transfers between devices, exchange(): return lax.all_to_all(values, axes, split_axis=0, concat_axis=0, tiled=True)  11.2 us
    all_to_all x1, waiting for transfers between devices, exchange(): return lax.all_to_all(values, axes, split_axis=0, concat_axis=0, tiled=True)  7.65 us
    pallas_call x1, Pallas kernels, middle(): pl.pallas_call(middle_kernel, out_shape=(shape((512, 256), BF), shape((8,...  2.74 us
  transfers between devices with their start and end apart: 1, of which 1 were waited for; matrix products, arithmetic and copies ran while one was open for 0% of the time, Pallas kernels for 2%

profile of v2, /device:TPU:1, one launch (start us, length us, event | category | flops | bytes accessed | tf_op | source)
XLA Modules:
  0.0 104.5 jit_solution(18272758485697336132)
XLA Ops:
  0.6 1.8 %shard_map.154 = (bf16[256,384]{1,0:T(8,128)(2,1)S(1)}, bf16[256,512]{1,0:T(8,128)(2,1)S(1)}, f32[256,512]{1,0:T(8,128)S(1)}, bf16[512,128]{1,0:T(8,128)(2,1)S(1...) custom-call(s32[2,128]{1,0:T(2,128)} %bitcast.30, ...), custom_call_target="tpu_custom_call" | custom-call | tf_op jit(solution)/shard_map/pallas_call | solution.py:203
  2.5 0.1 reshape.55
  2.5 38.2 %all_to_all.25 = bf16[128,2,384]{2,1,0:T(2,128)(2,1)S(1)} all-to-all(bf16[128,2,384]{2,1,0:T(2,128)(2,1)S(1)} %reshape.55), channel_id=1, replica_groups=mesh['z'=16,'x'=4,'core'=2,'y'=4] {'z','x','core'}, dimensions={0} | all-to-all | bytes 393216 | tf_op jit(solution)/shard_map/all_to_all | solution.py:296
  40.8 0.1 reshape.56.recv
  40.8 2.7 %shard_map.155 = (bf16[512,256]{1,0:T(8,128)(2,1)S(1)}, bf16[8,224,128]{2,1,0:T(8,128)(2,1)S(1)}) custom-call(s32[3,1,4]{2,1,0:T(1,128)S(1)} %get-tuple-element.27.index, bf16[256,384]{1,0:T(8,128)(2,1)S(1)} %reshape.56.recv, bf16[512,128]{1,0:T(8,128)(2,1)S(1)} %get-tuple-element.29.feat, bf16[12,128,128]{2,1,0:T(8,128)(2,1)S(1)} %get-tuple-element.30.tiles, ...), custom_call_target="tpu_custom_call" | custom-call | tf_op jit(solution)/shard_map/pallas_call | solution.py:222
  43.6 13.9 %all_to_all.26.parts = bf16[8,224,128]{2,1,0:T(8,128)(2,1)S(1)} all-to-all(bf16[8,224,128]{2,1,0:T(8,128)(2,1)S(1)} %get-tuple-element.39), channel_id=1, replica_groups=mesh['z'=16,'x'=4,'core'=2,'y'=4] {'x','core'}, dimensions={0} | all-to-all | bytes 917504 | tf_op jit(solution)/shard_map/all_to_all | solution.py:296
  57.5 0.3 shard_map.156
  57.7 8.3 %all_to_all.27.parts = bf16[4,40,128]{2,1,0:T(8,128)(2,1)S(1)} all-to-all(bf16[4,40,128]{2,1,0:T(8,128)(2,1)S(1)} %get-tuple-element.40), channel_id=1, replica_groups=mesh['z'=16,'x'=4,'core'=2,'y'=4] {'y'}, dimensions={0} | all-to-all | bytes 81920 | tf_op jit(solution)/shard_map/all_to_all | solution.py:296
  66.1 16.0 %all_to_all.28.recv.parts = bf16[16,72,128]{2,1,0:T(8,128)(2,1)S(1)} all-to-all(bf16[16,72,128]{2,1,0:T(8,128)(2,1)S(1)} %shard_map.157), channel_id=1, replica_groups=mesh['z'=16,'x'=4,'core'=2,'y'=4] {'z'}, dimensions={0} | all-to-all | bytes 589824 | tf_op jit(solution)/shard_map/all_to_all | solution.py:296
  82.1 0.8 shard_map.159
  82.8 11.2 %all-to-all-start.4 = ((bf16[32,40,128]{2,1,0:T(8,128)(2,1)}), bf16[32,40,128]{2,1,0:T(8,128)(2,1)S(1)}, u32[]{:S(2)}, u32[]{:S(2)}) async-start(bf16[32,40,128]{2,1,0:T(8,128)(2,1)} %shard_map.159), calls=%async_computation.4 | async-start | bytes 655360 | tf_op jit(solution)/shard_map/all_to_all | solution.py:296
  94.1 1.9 %shard_map.158 = bf16[172,512]{1,0:T(8,128)(2,1)} custom-call(s32[3,1,4]{2,1,0:T(1,128)S(1)} %get-tuple-element.27.index, bf16[16,72,128]{2,1,0:T(8,128)(2,1)S(1)} %all_to_all.28.recv.parts, bf16[512,256]{1,0:T(8,128)(2,1)S(1)} %get-tuple-element.42.hidden, bf16[12,128,128]{2,1,0:T(8,128)(2,1)S(1)} %get-tuple-element.30.tiles, ...), custom_call_target="tpu_custom_call" | custom-call | tf_op jit(solution)/shard_map/pallas_call | solution.py:239
  96.0 7.6 %all-to-all-done.4 = bf16[32,40,128]{2,1,0:T(8,128)(2,1)S(1)} async-done(((bf16[32,40,128]{2,1,0:T(8,128)(2,1)}), bf16[32,40,128]{2,1,0:T(8,128)(2,1)S(1)}, u32[]{:S(2)}, u32[]{:S(2)}) %all-to-all-start.4) | async-done | bytes 327712 | tf_op jit(solution)/shard_map/all_to_all | solution.py:296
  103.6 0.8 shard_map.160
  (1 shorter events, 0.0 us)
Async XLA Ops:
  82.8 20.8 %all-to-all-start.4 = ((bf16[32,40,128]{2,1,0:T(8,128)(2,1)}), bf16[32,40,128]{2,1,0:T(8,128)(2,1)S(1)}, u32[]{:S(2)}, u32[]{:S(2)}) async-start(bf16[32,40,128]{2,1,0:T(8,128)(2,1)} %shard_map.159), calls=%async_computation.4 | async-start | bytes 655360 | tf_op jit(solution)/shard_map/all_to_all | solution.py:296

commit v3 on v2

--- a/solution.py
+++ b/solution.py
@@ -7,8 +7,10 @@
 
 BF = jnp.bfloat16
 F32 = jnp.float32
-PLANE = ("x", "core", "y")
+EVERY = ("z", "x", "core", "y")
 WIDE = ("z", "x", "core")
+DIAGONALS = [[z * 4 + (g + z) % 4 for z in range(16)] for g in range(4)]
+PLANES = [[z * 32 + xc * 4 + (g + z) % 4 for xc in range(8) for g in range(4)] for z in range(16)]
 VM = pl.BlockSpec(memory_space=pltpu.VMEM)
 SM = pl.BlockSpec(memory_space=pltpu.SMEM)
 PARAMS = pltpu.CompilerParams(vmem_limit_bytes=32 * 1024 * 1024)
@@ -25,6 +27,10 @@
 def split(values):
     upper = values.astype(BF)
     return upper, (values - upper.astype(F32)).astype(BF)
+
+
+def place():
+    return lax.axis_index("z"), lax.axis_index("y")
 
 
 def before_kernel(*refs):
@@ -82,7 +88,7 @@
 
 def middle_kernel(
     index, recv, feat, tiles, pick, own_t, grad_t, w1s, w1n, bias, w2s_t, w2n_t,
-    hidden, out, ext, both, padded, wide_w, grads,
+    hidden, out, ext, both, padded, wide_w, grads, perm,
 ):
     for b in range(4):
         ext[b] = feat[b * 128 : (b + 1) * 128, :]
@@ -94,14 +100,18 @@
     pre = dot(both[:, 0:128], w1s[...]) + dot(both[:, 128:256], w1n[...]) + bias[...]
     hid = jnp.maximum(pre, 0.0).astype(BF)
     hidden[...] = hid
-    i = lax.broadcasted_iota(jnp.int32, (256, 256), 0)
-    j = lax.broadcasted_iota(jnp.int32, (256, 256), 1)
-    place = ((i // 2) % 16) * 16 + (i // 32) * 2 + i % 2
-    perm = jnp.where(j == place, 1.0, 0.0).astype(BF)
-    picked = dot(perm, dot(pick[...], hid).astype(BF)).astype(BF)
-    for p in range(8):
-        out[p, 160:192, :] = picked[p * 32 : (p + 1) * 32, 0:128]
-        out[p, 192:224, :] = picked[p * 32 : (p + 1) * 32, 128:256]
+    y = place()[1]
+    i = lax.broadcasted_iota(jnp.int32, (512, 128), 0)
+    z2 = ((y - (i >> 4)) & 3) + 4 * ((i >> 1) & 3)
+    source = ((i >> 3) & 1) * 256 + z2 * 16 + (i >> 6) * 2 + (i & 1)
+    lane = lax.broadcasted_iota(jnp.int32, (512, 128), 1)
+    for c in range(4):
+        perm[:, c * 128 : (c + 1) * 128] = jnp.where(source == lane + 128 * c, 1.0, 0.0).astype(BF)
+    picked = dot(pick[...], hid).astype(BF)
+    picked = jnp.concatenate([picked[:, 0:128], picked[:, 128:256]], axis=0)
+    picked = dot(perm[...], picked).astype(BF)
+    for p in range(32):
+        out[p, 0:16, :] = picked[p * 16 : (p + 1) * 16, :]
     padded[...] = jnp.zeros_like(padded)
     padded[0:172, :] = grad_t[...]
     wide_w[...] = jnp.zeros_like(wide_w)
@@ -129,35 +139,28 @@
         grads[base + 256 : base + 432, :] = self2[:, cols].astype(BF)
         grads[base + 432 : base + 608, :] = neigh2[:, cols].astype(BF)
         grads[base + 608 : base + 640, :] = jnp.zeros((32, 128), BF)
-    for p in range(8):
-        out[p, 0:160, :] = grads[p * 160 : (p + 1) * 160, :]
-
-
-def plane_kernel(parts, chunk, hidden):
-    total = parts[0, 0:160, :].astype(F32)
-    for p in range(1, 8):
-        total += parts[p, 0:160, :].astype(F32)
+    for p in range(32):
+        out[p, 16:56, :] = grads[p * 40 : (p + 1) * 40, :]
+
+
+def plane_kernel(parts, out, perm):
+    total = parts[0, 16:56, :].astype(F32)
+    for p in range(1, 32):
+        total += parts[p, 16:56, :].astype(F32)
     total = total.astype(BF)
-    for q in range(4):
-        chunk[q] = total[q * 40 : (q + 1) * 40, :]
-    i = lax.broadcasted_iota(jnp.int32, (256, 256), 0)
-    j = lax.broadcasted_iota(jnp.int32, (256, 256), 1)
-    place = ((i // 2) % 8) * 32 + (i // 16) * 2 + i % 2
-    perm = jnp.where(j == place, 1.0, 0.0).astype(BF)
-    for h in range(2):
-        rows = jnp.concatenate([parts[p, 160 + h * 32 : 192 + h * 32, :] for p in range(8)], axis=0)
-        hidden[:, h * 128 : (h + 1) * 128] = dot(perm, rows).astype(BF)
-
-
-def column_kernel(parts, hidden, out):
-    total = parts[0].astype(F32)
-    for p in range(1, 4):
-        total += parts[p].astype(F32)
-    total = total.astype(BF)
-    for z in range(16):
-        out[z, 0:16, :] = hidden[z * 16 : (z + 1) * 16, 0:128]
-        out[z, 16:32, :] = hidden[z * 16 : (z + 1) * 16, 128:256]
-        out[z, 32:72, :] = total
+    z, y = place()
+    i = lax.broadcasted_iota(jnp.int32, (512, 128), 0)
+    z2 = i >> 5
+    sender = ((i >> 1) & 7) * 4 + ((z2 + y - 2 * z) & 3)
+    source = sender * 16 + ((i >> 4) & 1) * 8 + (z2 >> 2) * 2 + (i & 1)
+    lane = lax.broadcasted_iota(jnp.int32, (512, 128), 1)
+    for c in range(4):
+        perm[:, c * 128 : (c + 1) * 128] = jnp.where(source == lane + 128 * c, 1.0, 0.0).astype(BF)
+    rows = jnp.concatenate([parts[p, 0:16, :] for p in range(32)], axis=0)
+    rows = dot(perm[...], rows).astype(BF)
+    for z2 in range(16):
+        out[z2, 0:32, :] = rows[z2 * 32 : (z2 + 1) * 32, :]
+        out[z2, 32:72, :] = total
 
 
 def layer_kernel(parts, out):
@@ -221,7 +224,7 @@
 def middle(index, recv, feat, tiles, pick, own_t, grad_t, w1s, w1n, bias, w2s_t, w2n_t):
     return pl.pallas_call(
         middle_kernel,
-        out_shape=(shape((512, 256), BF), shape((8, 224, 128), BF)),
+        out_shape=(shape((512, 256), BF), shape((32, 56, 128), BF)),
         in_specs=[SM] + [VM] * 11,
         out_specs=(VM, VM),
         scratch_shapes=[
@@ -230,6 +233,7 @@
             pltpu.VMEM((256, 512), BF),
             pltpu.VMEM((512, 256), BF),
             pltpu.VMEM((1280, 128), BF),
+            pltpu.VMEM((512, 512), BF),
         ],
         compiler_params=PARAMS,
     )(index, recv, feat, tiles, pick, own_t, grad_t, w1s, w1n, bias, w2s_t, w2n_t)
@@ -249,21 +253,12 @@
 def after_plane(parts):
     return pl.pallas_call(
         plane_kernel,
-        out_shape=(shape((4, 40, 128), BF), shape((256, 256), BF)),
+        out_shape=shape((16, 72, 128), BF),
         in_specs=[VM],
-        out_specs=(VM, VM),
+        out_specs=VM,
+        scratch_shapes=[pltpu.VMEM((512, 512), BF)],
         compiler_params=PARAMS,
     )(parts)
-
-
-def after_column(parts, hidden):
-    return pl.pallas_call(
-        column_kernel,
-        out_shape=shape((16, 72, 128), BF),
-        in_specs=[VM, VM],
-        out_specs=VM,
-        compiler_params=PARAMS,
-    )(parts, hidden)
 
 
 def after_layers(parts):
@@ -292,8 +287,8 @@
     )(total)
 
 
-def exchange(values, axes):
-    return lax.all_to_all(values, axes, split_axis=0, concat_axis=0, tiled=True)
+def exchange(values, axes, groups=None):
+    return lax.all_to_all(values, axes, split_axis=0, concat_axis=0, axis_index_groups=groups, tiled=True)
 
 
 def shards(
@@ -328,9 +323,8 @@
         index, recv1, feat, tiles, pick, own_t, grad_t,
         w1s, w1n, bias, w2s_t, w2n_t,
     )
-    chunk, passing = after_plane(exchange(parts, ("x", "core")))
-    recv2 = exchange(after_column(exchange(chunk, "y"), passing), "z")
-    total = exchange(after_layers(recv2), PLANE)
+    recv2 = exchange(after_plane(exchange(parts, EVERY, PLANES)), ("z", "y"), DIAGONALS)
+    total = exchange(after_layers(recv2), EVERY, PLANES)
     logits_t = scores(index, recv2, hidden, tiles, w2s_t, w2n_t)
     self1, neigh1, bias1, self2_t, neigh2_t = finish(total.reshape(1280, 128))
     logits = jnp.swapaxes(logits_t, 0, 1).reshape(1, 1, 512, 172)

time: 105 us -> 106 us (level)
  blocking collectives: 76.4 us -> 81.2 us
  starting transfers between devices: 11.2 us -> 7.47 us
    all_to_all x4 -> x3, blocking collectives: 76.4 us -> 81.2 us  [exchange(): lax.all_to_all(values, axes, split_axis=0, concat_axis=0, axis_index_grou...]
    all_to_all x1, starting transfers between devices: 11.2 us -> 7.47 us  [exchange(): lax.all_to_all(values, axes, split_axis=0, concat_axis=0, axis_index_grou...]
    pallas_call x3 -> x2, Pallas kernels: 3.03 us -> 3.51 us  [the longest x1 3 us: middle(): pl.pallas_call(middle_kernel, out_shape=(shape((512, 256), BF), shape((32...]
where the time goes in v3:
time: 106 us
  blocking collectives  81.2 us (77%)
  Pallas kernels  8.82 us (8%)
  waiting for transfers between devices  7.56 us (7%)
  starting transfers between devices  7.47 us (7%)
    all_to_all x3, blocking collectives, exchange(): lax.all_to_all(values, axes, split_axis=0, concat_axis=0, axis_index_grou...  81.2 us
    all_to_all x1, waiting for transfers between devices, exchange(): lax.all_to_all(values, axes, split_axis=0, concat_axis=0, axis_index_grou...  7.56 us
    all_to_all x1, starting transfers between devices, exchange(): lax.all_to_all(values, axes, split_axis=0, concat_axis=0, axis_index_grou...  7.47 us
    pallas_call x1, Pallas kernels, middle(): pl.pallas_call(middle_kernel, out_shape=(shape((512, 256), BF), shape((32...  3 us
  transfers between devices with their start and end apart: 1, of which 1 were waited for; matrix products, arithmetic and copies ran while one was open for 0% of the time, Pallas kernels for 2%

profile of v3, /device:TPU:1, one launch (start us, length us, event | category | flops | bytes accessed | tf_op | source)
XLA Modules:
  0.0 105.9 jit_solution(10457809590922601753)
XLA Ops:
  0.6 1.8 %shard_map.154 = (bf16[256,384]{1,0:T(8,128)(2,1)S(1)}, bf16[256,512]{1,0:T(8,128)(2,1)S(1)}, f32[256,512]{1,0:T(8,128)S(1)}, bf16[512,128]{1,0:T(8,128)(2,1)S(1...) custom-call(s32[2,128]{1,0:T(2,128)} %bitcast.30, ...), custom_call_target="tpu_custom_call" | custom-call | tf_op jit(solution)/shard_map/pallas_call | solution.py:206
  2.5 0.1 reshape.55
  2.5 38.2 %all_to_all.20 = bf16[128,2,384]{2,1,0:T(2,128)(2,1)S(1)} all-to-all(bf16[128,2,384]{2,1,0:T(2,128)(2,1)S(1)} %reshape.55), channel_id=1, replica_groups=mesh['z'=16,'x'=4,'core'=2,'y'=4] {'z','x','core'}, dimensions={0} | all-to-all | bytes 393216 | tf_op jit(solution)/shard_map/all_to_all | solution.py:291
  40.8 0.1 reshape.56.recv
  40.8 3.0 %shard_map.155 = (bf16[512,256]{1,0:T(8,128)(2,1)S(1)}, bf16[32,56,128]{2,1,0:T(8,128)(2,1)S(1)}) custom-call(s32[3,1,4]{2,1,0:T(1,128)S(1)} %get-tuple-element.25.index, bf16[256,384]{1,0:T(8,128)(2,1)S(1)} %reshape.56.recv, bf16[512,128]{1,0:T(8,128)(2,1)S(1)} %get-tuple-element.27.feat, bf16[12,128,128]{2,1,0:T(8,128)(2,1)S(1)} %get-tuple-element.28.tiles, ...), custom_call_target="tpu_custom_call" | custom-call | tf_op jit(solution)/shard_map/pallas_call | solution.py:225
  43.9 18.5 %all_to_all.21.parts = bf16[32,56,128]{2,1,0:T(8,128)(2,1)S(1)} all-to-all(bf16[32,56,128]{2,1,0:T(8,128)(2,1)S(1)} %get-tuple-element.37), channel_id=1, replica_groups={{0,1,2,3,4,5,6,7,8,9,10,11,12,13,14,15,16,17,18,19,20,21,22,23,24,25,26..., dimensions={0} | all-to-all | bytes 917504 | tf_op jit(solution)/shard_map/all_to_all | solution.py:291
  62.3 0.5 shard_map.156
  62.8 24.5 %all_to_all.22.recv.parts = bf16[16,72,128]{2,1,0:T(8,128)(2,1)S(1)} all-to-all(bf16[16,72,128]{2,1,0:T(8,128)(2,1)S(1)} %shard_map.156), channel_id=1, replica_groups={{0,33,66,99,128,161,194,227,256,289,322,355,384,417,450,483},{1,34,67,9..., dimensions={0} | all-to-all | bytes 589824 | tf_op jit(solution)/shard_map/all_to_all | solution.py:291
  87.3 0.8 shard_map.158
  88.1 7.5 %all-to-all-start.3 = ((bf16[32,40,128]{2,1,0:T(8,128)(2,1)}), bf16[32,40,128]{2,1,0:T(8,128)(2,1)S(1)}, u32[]{:S(2)}, u32[]{:S(2)}) async-start(bf16[32,40,128]{2,1,0:T(8,128)(2,1)} %shard_map.158), calls=%async_computation.3 | async-start | bytes 655360 | tf_op jit(solution)/shard_map/all_to_all | solution.py:291
  95.6 1.9 %shard_map.157 = bf16[172,512]{1,0:T(8,128)(2,1)} custom-call(s32[3,1,4]{2,1,0:T(1,128)S(1)} %get-tuple-element.25.index, bf16[16,72,128]{2,1,0:T(8,128)(2,1)S(1)} %all_to_all.22.recv.parts, bf16[512,256]{1,0:T(8,128)(2,1)S(1)} %get-tuple-element.38.hidden, bf16[12,128,128]{2,1,0:T(8,128)(2,1)S(1)} %get-tuple-element.28.tiles, ...), custom_call_target="tpu_custom_call" | custom-call | tf_op jit(solution)/shard_map/pallas_call | solution.py:243
  97.5 7.6 %all-to-all-done.3 = bf16[32,40,128]{2,1,0:T(8,128)(2,1)S(1)} async-done(((bf16[32,40,128]{2,1,0:T(8,128)(2,1)}), bf16[32,40,128]{2,1,0:T(8,128)(2,1)S(1)}, u32[]{:S(2)}, u32[]{:S(2)}) %all-to-all-start.3) | async-done | bytes 327712 | tf_op jit(solution)/shard_map/all_to_all | solution.py:291
  105.0 0.8 shard_map.159
Async XLA Ops:
  88.1 16.9 %all-to-all-start.3 = ((bf16[32,40,128]{2,1,0:T(8,128)(2,1)}), bf16[32,40,128]{2,1,0:T(8,128)(2,1)S(1)}, u32[]{:S(2)}, u32[]{:S(2)}) async-start(bf16[32,40,128]{2,1,0:T(8,128)(2,1)} %shard_map.158), calls=%async_computation.3 | async-start | bytes 655360 | tf_op jit(solution)/shard_map/all_to_all | solution.py:291

commit v4 on v2

--- a/solution.py
+++ b/solution.py
@@ -25,6 +25,10 @@
 def split(values):
     upper = values.astype(BF)
     return upper, (values - upper.astype(F32)).astype(BF)
+
+
+def place():
+    return lax.axis_index("y")
 
 
 def before_kernel(*refs):
@@ -82,31 +86,42 @@
 
 def middle_kernel(
     index, recv, feat, tiles, pick, own_t, grad_t, w1s, w1n, bias, w2s_t, w2n_t,
-    hidden, out, ext, both, padded, wide_w, grads,
+    hidden, project, out, ext, both, padded, wide_w, grads,
 ):
     for b in range(4):
         ext[b] = feat[b * 128 : (b + 1) * 128, :]
     for b in range(2):
         ext[4 + b] = recv[b * 128 : (b + 1) * 128, 0:128]
     both[:, 0:128] = feat[...]
+    wide_w[...] = jnp.zeros_like(wide_w)
     for b in range(4):
         both[b * 128 : (b + 1) * 128, 128:256] = gather_tiles(index, tiles, ext, b)
     pre = dot(both[:, 0:128], w1s[...]) + dot(both[:, 128:256], w1n[...]) + bias[...]
     hid = jnp.maximum(pre, 0.0).astype(BF)
     hidden[...] = hid
+    wide_w[256 : 256 + 172, :] = w2n_t[...]
+    wide_w[256 + 192 : 256 + 236, :] = w2n_t[128:172, :]
+    near = dot_nt(hid, wide_w[256:512, :]).astype(BF)
+    project[...] = near
+    picked = dot(pick[...], near).astype(BF)
     i = lax.broadcasted_iota(jnp.int32, (256, 256), 0)
     j = lax.broadcasted_iota(jnp.int32, (256, 256), 1)
-    place = ((i // 2) % 16) * 16 + (i // 32) * 2 + i % 2
-    perm = jnp.where(j == place, 1.0, 0.0).astype(BF)
-    picked = dot(perm, dot(pick[...], hid).astype(BF)).astype(BF)
+    place_of = ((i >> 1) & 15) * 16 + (i >> 5) * 2 + (i & 1)
+    heads = dot(jnp.where(j == place_of, 1.0, 0.0).astype(BF), picked[:, 0:128]).astype(BF)
+    i = lax.broadcasted_iota(jnp.int32, (128, 256), 0)
+    j = lax.broadcasted_iota(jnp.int32, (128, 256), 1)
+    place_of = (i & 15) * 16 + (i >> 4) * 2
+    tail0 = dot(jnp.where(j == place_of, 1.0, 0.0).astype(BF), picked[:, 128:256])
+    tail1 = dot(jnp.where(j == place_of + 1, 1.0, 0.0).astype(BF), picked[:, 128:256])
+    lane = lax.broadcasted_iota(jnp.int32, (128, 128), 1)
+    tails = jnp.where(lane < 64, tail0, tail1).astype(BF)
+    y = place()
     for p in range(8):
-        out[p, 160:192, :] = picked[p * 32 : (p + 1) * 32, 0:128]
-        out[p, 192:224, :] = picked[p * 32 : (p + 1) * 32, 128:256]
+        out[p * 4 + y, 0:32, :] = heads[p * 32 : (p + 1) * 32, :]
+        out[p * 4 + y, 32:48, :] = tails[p * 16 : (p + 1) * 16, :]
     padded[...] = jnp.zeros_like(padded)
     padded[0:172, :] = grad_t[...]
-    wide_w[...] = jnp.zeros_like(wide_w)
     wide_w[0:172, :] = w2s_t[...]
-    wide_w[256 : 256 + 172, :] = w2n_t[...]
     returned_t = recv[:, 128:384].astype(F32).T.astype(BF)
     back_t = own_t[...] + dot(returned_t, pick[...])
     upper_t, lower_t = split(back_t)
@@ -129,57 +144,65 @@
         grads[base + 256 : base + 432, :] = self2[:, cols].astype(BF)
         grads[base + 432 : base + 608, :] = neigh2[:, cols].astype(BF)
         grads[base + 608 : base + 640, :] = jnp.zeros((32, 128), BF)
-    for p in range(8):
-        out[p, 0:160, :] = grads[p * 160 : (p + 1) * 160, :]
-
-
-def plane_kernel(parts, chunk, hidden):
-    total = parts[0, 0:160, :].astype(F32)
-    for p in range(1, 8):
-        total += parts[p, 0:160, :].astype(F32)
+    for p in range(32):
+        out[p, 48:88, :] = grads[p * 40 : (p + 1) * 40, :]
+
+
+def plane_kernel(parts, out):
+    total = parts[0, 48:88, :].astype(F32)
+    for p in range(1, 32):
+        total += parts[p, 48:88, :].astype(F32)
     total = total.astype(BF)
-    for q in range(4):
-        chunk[q] = total[q * 40 : (q + 1) * 40, :]
+    y = place()
     i = lax.broadcasted_iota(jnp.int32, (256, 256), 0)
     j = lax.broadcasted_iota(jnp.int32, (256, 256), 1)
-    place = ((i // 2) % 8) * 32 + (i // 16) * 2 + i % 2
-    perm = jnp.where(j == place, 1.0, 0.0).astype(BF)
-    for h in range(2):
-        rows = jnp.concatenate([parts[p, 160 + h * 32 : 192 + h * 32, :] for p in range(8)], axis=0)
-        hidden[:, h * 128 : (h + 1) * 128] = dot(perm, rows).astype(BF)
-
-
-def column_kernel(parts, hidden, out):
-    total = parts[0].astype(F32)
-    for p in range(1, 4):
-        total += parts[p].astype(F32)
-    total = total.astype(BF)
+    place_of = ((i >> 1) & 7) * 32 + (i >> 4) * 2 + (i & 1)
+    heads = jnp.concatenate([parts[p * 4 + y, 0:32, :] for p in range(8)], axis=0)
+    heads = dot(jnp.where(j == place_of, 1.0, 0.0).astype(BF), heads).astype(BF)
+    i = lax.broadcasted_iota(jnp.int32, (128, 128), 0)
+    j = lax.broadcasted_iota(jnp.int32, (128, 128), 1)
+    place_of = (i & 7) * 16 + (i >> 3)
+    tails = jnp.concatenate([parts[p * 4 + y, 32:48, :] for p in range(8)], axis=0)
+    tails = dot(jnp.where(j == place_of, 1.0, 0.0).astype(BF), tails).astype(BF)
     for z in range(16):
-        out[z, 0:16, :] = hidden[z * 16 : (z + 1) * 16, 0:128]
-        out[z, 16:32, :] = hidden[z * 16 : (z + 1) * 16, 128:256]
-        out[z, 32:72, :] = total
+        out[z, 0:16, :] = heads[z * 16 : (z + 1) * 16, :]
+        out[z, 16:24, :] = tails[z * 8 : (z + 1) * 8, :]
+        out[z, 24:64, :] = total
 
 
 def layer_kernel(parts, out):
-    total = parts[0, 32:72, :].astype(F32)
+    total = parts[0, 24:64, :].astype(F32)
     for p in range(1, 16):
-        total += parts[p, 32:72, :].astype(F32)
+        total += parts[p, 24:64, :].astype(F32)
     total = total.astype(BF)
     for p in range(32):
         out[p] = total
 
 
-def logits_kernel(index, recv, hidden, tiles, w2s_t, w2n_t, out_t, ext, agg):
-    for b in range(4):
-        ext[b] = hidden[b * 128 : (b + 1) * 128, :]
+def logits_kernel(index, recv, hidden, project, tiles, w2s_t, out_t, ext, wide_w, result):
+    for b in range(4):
+        ext[b] = project[b * 128 : (b + 1) * 128, :]
+    tails = jnp.concatenate([recv[z, 16:24, :] for z in range(16)], axis=0)
+    i = lax.broadcasted_iota(jnp.int32, (256, 128), 0)
+    j = lax.broadcasted_iota(jnp.int32, (256, 128), 1)
+    tails = dot(jnp.where(j == (i >> 1), 1.0, 0.0).astype(BF), tails)
+    m = lax.broadcasted_iota(jnp.int32, (128, 128), 0)
+    n = lax.broadcasted_iota(jnp.int32, (128, 128), 1)
+    other = dot(tails.astype(BF), jnp.where(n == (m ^ 64), 1.0, 0.0).astype(BF))
+    tails = jnp.where((i & 1) == 0, tails, other).astype(BF)
     for z in range(16):
-        rows = slice((z % 8) * 16, (z % 8) * 16 + 16)
-        ext[4 + z // 8, rows, 0:128] = recv[z, 0:16, :]
-        ext[4 + z // 8, rows, 128:256] = recv[z, 16:32, :]
-    for b in range(4):
-        agg[b * 128 : (b + 1) * 128, :] = gather_tiles(index, tiles, ext, b)
-    scores = dot_nt(w2s_t[...], hidden[...]) + dot_nt(w2n_t[...], agg[...])
-    out_t[...] = scores.astype(BF)
+        ext[4 + z // 8, (z % 8) * 16 : (z % 8) * 16 + 16, 0:128] = recv[z, 0:16, :]
+    for b in range(2):
+        ext[4 + b, :, 128:256] = tails[b * 128 : (b + 1) * 128, :]
+    wide_w[...] = jnp.zeros_like(wide_w)
+    wide_w[0:172, :] = w2s_t[...]
+    for b in range(4):
+        rows = slice(b * 128, (b + 1) * 128)
+        total = dot_nt(hidden[rows, :], wide_w[...])
+        for k in range(3):
+            total += dot(tiles[b * 3 + k], ext[index[k, 0, b]])
+        result[:, rows] = total.T
+    out_t[...] = result[0:172, :].astype(BF)
 
 
 def finish_kernel(total, self1, neigh1, bias, self2_t, neigh2_t):
@@ -221,9 +244,9 @@
 def middle(index, recv, feat, tiles, pick, own_t, grad_t, w1s, w1n, bias, w2s_t, w2n_t):
     return pl.pallas_call(
         middle_kernel,
-        out_shape=(shape((512, 256), BF), shape((8, 224, 128), BF)),
+        out_shape=(shape((512, 256), BF), shape((512, 256), BF), shape((32, 88, 128), BF)),
         in_specs=[SM] + [VM] * 11,
-        out_specs=(VM, VM),
+        out_specs=(VM, VM, VM),
         scratch_shapes=[
             pltpu.VMEM((6, 128, 128), BF),
             pltpu.VMEM((512, 256), BF),
@@ -235,35 +258,29 @@
     )(index, recv, feat, tiles, pick, own_t, grad_t, w1s, w1n, bias, w2s_t, w2n_t)
 
 
-def scores(index, recv, hidden, tiles, w2s_t, w2n_t):
+def scores(index, recv, hidden, project, tiles, w2s_t):
     return pl.pallas_call(
         logits_kernel,
         out_shape=shape((172, 512), BF),
         in_specs=[SM] + [VM] * 5,
         out_specs=VM,
-        scratch_shapes=[pltpu.VMEM((6, 128, 256), BF), pltpu.VMEM((512, 256), BF)],
-        compiler_params=PARAMS,
-    )(index, recv, hidden, tiles, w2s_t, w2n_t)
+        scratch_shapes=[
+            pltpu.VMEM((6, 128, 256), BF),
+            pltpu.VMEM((256, 256), BF),
+            pltpu.VMEM((256, 512), F32),
+        ],
+        compiler_params=PARAMS,
+    )(index, recv, hidden, project, tiles, w2s_t)
 
 
 def after_plane(parts):
     return pl.pallas_call(
         plane_kernel,
-        out_shape=(shape((4, 40, 128), BF), shape((256, 256), BF)),
+        out_shape=shape((16, 64, 128), BF),
         in_specs=[VM],
-        out_specs=(VM, VM),
+        out_specs=VM,
         compiler_params=PARAMS,
     )(parts)
-
-
-def after_column(parts, hidden):
-    return pl.pallas_call(
-        column_kernel,
-        out_shape=shape((16, 72, 128), BF),
-        in_specs=[VM, VM],
-        out_specs=VM,
-        compiler_params=PARAMS,
-    )(parts, hidden)
 
 
 def after_layers(parts):
@@ -324,14 +341,13 @@
         first_layer_self_weight, first_layer_neighbour_weight, bias, w2s_t, w2n_t, index,
     )
     recv1 = exchange(send1.reshape(128, 2, 384), WIDE).reshape(256, 384)
-    hidden, parts = middle(
+    hidden, project, parts = middle(
         index, recv1, feat, tiles, pick, own_t, grad_t,
         w1s, w1n, bias, w2s_t, w2n_t,
     )
-    chunk, passing = after_plane(exchange(parts, ("x", "core")))
-    recv2 = exchange(after_column(exchange(chunk, "y"), passing), "z")
+    recv2 = exchange(after_plane(exchange(parts, PLANE)), "z")
     total = exchange(after_layers(recv2), PLANE)
-    logits_t = scores(index, recv2, hidden, tiles, w2s_t, w2n_t)
+    logits_t = scores(index, recv2, hidden, project, tiles, w2s_t)
     self1, neigh1, bias1, self2_t, neigh2_t = finish(total.reshape(1280, 128))
     logits = jnp.swapaxes(logits_t, 0, 1).reshape(1, 1, 512, 172)
     return (

time: 105 us -> 102 us (0.971)
  blocking collectives: 76.4 us -> 74.7 us
    all_to_all x4 -> x3, blocking collectives: 76.4 us -> 74.7 us  [exchange(): return lax.all_to_all(values, axes, split_axis=0, concat_axis=0, tiled=True)]
    pallas_call x3 -> x2, Pallas kernels: 3.03 us -> 3.06 us  [the longest x1 2.87 us: middle(): pl.pallas_call(middle_kernel, out_shape=(shape((512, 256), BF), shape((51...]
where the time goes in v4:
time: 102 us
  blocking collectives  74.7 us (73%)
  starting transfers between devices  10.2 us (10%)
  Pallas kernels  8.64 us (8%)
  waiting for transfers between devices  7.39 us (7%)
    all_to_all x3, blocking collectives, exchange(): return lax.all_to_all(values, axes, split_axis=0, concat_axis=0, tiled=True)  74.7 us
    all_to_all x1, starting transfers between devices, exchange(): return lax.all_to_all(values, axes, split_axis=0, concat_axis=0, tiled=True)  10.2 us
    all_to_all x1, waiting for transfers between devices, exchange(): return lax.all_to_all(values, axes, split_axis=0, concat_axis=0, tiled=True)  7.39 us
    pallas_call x1, Pallas kernels, middle(): pl.pallas_call(middle_kernel, out_shape=(shape((512, 256), BF), shape((51...  2.87 us
    pallas_call x1, Pallas kernels, scores(): pl.pallas_call(logits_kernel, out_shape=shape((172, 512), BF), in_specs=[...  2.16 us
  transfers between devices with their start and end apart: 1, of which 1 were waited for; matrix products, arithmetic and copies ran while one was open for 0% of the time, Pallas kernels for 2%

profile of v4, /device:TPU:1, one launch (start us, length us, event | category | flops | bytes accessed | tf_op | source)
XLA Modules:
  0.0 101.8 jit_solution(1096667373539415851)
XLA Ops:
  0.6 1.8 %shard_map.154 = (bf16[256,384]{1,0:T(8,128)(2,1)S(1)}, bf16[256,512]{1,0:T(8,128)(2,1)S(1)}, f32[256,512]{1,0:T(8,128)S(1)}, bf16[512,128]{1,0:T(8,128)(2,1)S(1...) custom-call(s32[2,128]{1,0:T(2,128)} %bitcast.30, ...), custom_call_target="tpu_custom_call" | custom-call | tf_op jit(solution)/shard_map/pallas_call | solution.py:226
  2.5 0.1 reshape.55
  2.5 38.2 %all_to_all.20 = bf16[128,2,384]{2,1,0:T(2,128)(2,1)S(1)} all-to-all(bf16[128,2,384]{2,1,0:T(2,128)(2,1)S(1)} %reshape.55), channel_id=1, replica_groups=mesh['z'=16,'x'=4,'core'=2,'y'=4] {'z','x','core'}, dimensions={0} | all-to-all | bytes 393216 | tf_op jit(solution)/shard_map/all_to_all | solution.py:313
  40.8 0.1 reshape.56.recv
  40.8 2.9 %shard_map.155 = (bf16[512,256]{1,0:T(8,128)(2,1)S(1)}, bf16[512,256]{1,0:T(8,128)(2,1)S(1)}, bf16[32,88,128]{2,1,0:T(8,128)(2,1)S(1)}) custom-call(s32[3,1,4]{2,1,0:T(1,128)S(1)} %get-tuple-element.26.index, bf16[256,384]{1,0:T(8,128)(2,1)S(1)} %reshape.56.recv, bf16[512,128]{1,0:T(8,128)(2,1)S(1)} %get-tuple-element.28.feat, ...), custom_call_target="tpu_custom_call" | custom-call | tf_op jit(solution)/shard_map/pallas_call | solution.py:245
  43.7 20.8 %all_to_all.21.parts = bf16[32,88,128]{2,1,0:T(8,128)(2,1)S(1)} all-to-all(bf16[32,88,128]{2,1,0:T(8,128)(2,1)S(1)} %get-tuple-element.38), channel_id=1, replica_groups=mesh['z'=16,'x'=4,'core'=2,'y'=4] {'x','core','y'}, dimensions={0} | all-to-all | bytes 1441792 | tf_op jit(solution)/shard_map/all_to_all | solution.py:313
  64.5 0.2 shard_map.156
  64.7 15.7 %all_to_all.22.recv.parts = bf16[16,64,128]{2,1,0:T(8,128)(2,1)S(1)} all-to-all(bf16[16,64,128]{2,1,0:T(8,128)(2,1)S(1)} %shard_map.156), channel_id=1, replica_groups=mesh['z'=16,'x'=4,'core'=2,'y'=4] {'z'}, dimensions={0} | all-to-all | bytes 524288 | tf_op jit(solution)/shard_map/all_to_all | solution.py:313
  80.4 0.8 shard_map.158
  81.2 10.2 %all-to-all-start.3 = ((bf16[32,40,128]{2,1,0:T(8,128)(2,1)}), bf16[32,40,128]{2,1,0:T(8,128)(2,1)S(1)}, u32[]{:S(2)}, u32[]{:S(2)}) async-start(bf16[32,40,128]{2,1,0:T(8,128)(2,1)} %shard_map.158), calls=%async_computation.3 | async-start | bytes 655360 | tf_op jit(solution)/shard_map/all_to_all | solution.py:313
  91.4 2.2 %shard_map.157 = bf16[172,512]{1,0:T(8,128)(2,1)} custom-call(s32[3,1,4]{2,1,0:T(1,128)S(1)} %get-tuple-element.26.index, bf16[16,64,128]{2,1,0:T(8,128)(2,1)S(1)} %all_to_all.22.recv.parts, bf16[512,256]{1,0:T(8,128)(2,1)S(1)} %get-tuple-element.39.hidden, bf16[512,256]{1,0:T(8,128)(2,1)S(1)} %get-tuple-element.40.project, ...), custom_call_target="tpu_custom_call" | custom-call | tf_op jit(solution)/shard_map/pallas_call | solution.py:262
  93.5 7.4 %all-to-all-done.3 = bf16[32,40,128]{2,1,0:T(8,128)(2,1)S(1)} async-done(((bf16[32,40,128]{2,1,0:T(8,128)(2,1)}), bf16[32,40,128]{2,1,0:T(8,128)(2,1)S(1)}, u32[]{:S(2)}, u32[]{:S(2)}) %all-to-all-start.3) | async-done | bytes 327712 | tf_op jit(solution)/shard_map/all_to_all | solution.py:313
  100.9 0.8 shard_map.159
Async XLA Ops:
  81.2 19.8 %all-to-all-start.3 = ((bf16[32,40,128]{2,1,0:T(8,128)(2,1)}), bf16[32,40,128]{2,1,0:T(8,128)(2,1)S(1)}, u32[]{:S(2)}, u32[]{:S(2)}) async-start(bf16[32,40,128]{2,1,0:T(8,128)(2,1)} %shard_map.158), calls=%async_computation.3 | async-start | bytes 655360 | tf_op jit(solution)/shard_map/all_to_all | solution.py:313

commit v5 on v3

v5 whole, which is shorter than its diff:
```python
import jax
import jax.numpy as jnp
from jax import lax
from jax.experimental import pallas as pl
from jax.experimental.pallas import tpu as pltpu
from jax.sharding import Mesh, PartitionSpec as P

BF = jnp.bfloat16
F32 = jnp.float32
PLANE = ("x", "core", "y")
WIDE = ("z", "x", "core")
VM = pl.BlockSpec(memory_space=pltpu.VMEM)
SM = pl.BlockSpec(memory_space=pltpu.SMEM)
PARAMS = pltpu.CompilerParams(vmem_limit_bytes=32 * 1024 * 1024)


def dot(a, b):
    return jnp.dot(a, b, preferred_element_type=F32)


def dot_nt(a, b):
    return lax.dot_general(a, b, (((1,), (1,)), ((), ())), preferred_element_type=F32)


def split(values):
    upper = values.astype(BF)
    return upper, (values - upper.astype(F32)).astype(BF)


def place():
    return lax.axis_index("y")


def before_kernel(*refs):
    rows_in, counts_in = refs[0:2]
    send, pick, pick_out, own_t = refs[11:15]
    feat, grad_t, tiles = refs[15:18]
    rows, counts, index, acc, padded, sems = refs[24:30]
    pairs = [(rows_in, rows), (counts_in, counts)] + list(zip(refs[2:11], refs[15:24])) + [(refs[10], index)]
    copies = [pltpu.make_async_copy(a, b, sems.at[i]) for i, (a, b) in enumerate(pairs)]
    for copy in copies:
        copy.start()
    acc[...] = jnp.zeros_like(acc)
    padded[...] = jnp.zeros_like(padded)
    i = lax.broadcasted_iota(jnp.int32, (256, 256), 0)
    j = lax.broadcasted_iota(jnp.int32, (256, 256), 1)
    orders = (((i & 1) * 128 + (i >> 1), pick), (((i >> 4) & 1) * 128 + (i & 15) * 8 + (i >> 5), pick_out))
    copies[0].wait()
    copies[1].wait()
    slot = lax.broadcasted_iota(jnp.int32, (2, 128), 0)
    wanted = jnp.where(slot < counts[...], rows[...], 512)
    by_slot = jnp.concatenate([wanted[0:1, :], wanted[1:2, :]], axis=1)
    wide_rows = jnp.broadcast_to(by_slot, (128, 256))
    half = wide_rows // 2
    low = wide_rows - half * 2
    half = half.astype(F32).astype(BF)
    low = low.astype(F32).astype(BF)
    lane = lax.broadcasted_iota(jnp.int32, (256, 128), 1).astype(F32)
    for place_of, target in orders:
        perm = jnp.where(j == place_of, 1.0, 0.0).astype(BF)
        column = 2.0 * dot_nt(perm, half) + dot_nt(perm, low)
        if target is pick:
            live = jnp.where(column < 512.0, 1.0, 0.0)
        for c in range(4):
            target[:, c * 128 : (c + 1) * 128] = jnp.where(column == lane + 128.0 * c, 1.0, 0.0).astype(BF)
    copies[2].wait()
    send[:, 0:128] = dot(pick[...], feat[...]).astype(BF)
    copies[3].wait()
    padded[0:172, :] = grad_t[...]
    copies[4].wait()
    copies[11].wait()
    for b in range(4):
        part = padded[:, b * 128 : (b + 1) * 128]
        for k in range(3):
            e = index[k, 0, b]
            acc[e] += dot(part, tiles[b * 3 + k])
    for b in range(4):
        own_t[:, b * 128 : (b + 1) * 128] = acc[b]
    for b in range(2):
        rows_of = slice(b * 128, (b + 1) * 128)
        back = acc[4 + b].T
        tail = jnp.where(lane[rows_of, :] == 44.0, live[rows_of, :], back[:, 128:256])
        send[rows_of, 128:256] = back[:, 0:128].astype(BF)
        send[rows_of, 256:384] = tail.astype(BF)
    for copy in copies[5:11]:
        copy.wait()


def gather_tiles(index, tiles, ext, b):
    total = dot(tiles[b * 3], ext[index[0, 0, b]])
    total += dot(tiles[b * 3 + 1], ext[index[1, 0, b]])
    total += dot(tiles[b * 3 + 2], ext[index[2, 0, b]])
    return total.astype(BF)


def middle_kernel(
    index, recv, feat, tiles, pick, pick_out, own_t, grad_t, w1s, w1n, bias, w2s_t, w2n_t,
    hidden, out, ext, both, padded, wide_w,
):
    for b in range(4):
        ext[b] = feat[b * 128 : (b + 1) * 128, :]
    for b in range(2):
        ext[4 + b] = recv[b * 128 : (b + 1) * 128, 0:128]
    both[:, 0:128] = feat[...]
    wide_w[...] = jnp.zeros_like(wide_w)
    for b in range(4):
        both[b * 128 : (b + 1) * 128, 128:256] = gather_tiles(index, tiles, ext, b)
    picked = dot(pick_out[...], both[:, 128:256]).astype(BF)
    y = place()
    for p in range(8):
        out[p * 4 + y, 0:32, :] = picked[p * 32 : (p + 1) * 32, :]
    pre = dot(both[:, 0:128], w1s[...]) + dot(both[:, 128:256], w1n[...]) + bias[...]
    hid = jnp.maximum(pre, 0.0).astype(BF)
    hidden[...] = hid
    padded[...] = jnp.zeros_like(padded)
    padded[0:172, :] = grad_t[...]
    wide_w[0:172, :] = w2s_t[...]
    wide_w[256 : 256 + 172, :] = w2n_t[...]
    returned_t = recv[:, 128:384].astype(F32).T.astype(BF)
    back_t = own_t[...] + dot(returned_t, pick[...])
    upper_t, lower_t = split(back_t)
    upper, lower = split(back_t.T)
    grad = padded[...]
    grad_hidden = dot(grad.astype(F32).T.astype(BF), wide_w[0:256, :])
    grad_hidden += dot(upper, wide_w[256:512, :]) + dot(lower, wide_w[256:512, :])
    grad_pre = jnp.where(pre > 0, grad_hidden, 0.0).astype(BF)
    first = dot(both[...].astype(F32).T.astype(BF), grad_pre)
    bias_sum = jnp.sum(grad_pre.astype(F32), axis=0, keepdims=True)
    self2 = dot(grad, hid)
    neigh2 = dot(upper_t, hid) + dot(lower_t, hid)
    row = lax.broadcasted_iota(jnp.int32, (176, 256), 0)
    self2 = jnp.where(row == 172, bias_sum, self2[0:176, :])
    neigh2 = neigh2[0:176, :]
    rest = jnp.concatenate([self2, neigh2, jnp.zeros((32, 256), F32)], axis=0)
    grads = jnp.concatenate([first, rest], axis=0).astype(BF)
    for p in range(32):
        out[p, 32:72, :] = grads[(p % 16) * 40 : (p % 16) * 40 + 40, (p // 16) * 128 : (p // 16) * 128 + 128]


def plane_kernel(parts, out):
    total = parts[0, 32:72, :].astype(F32)
    for p in range(1, 32):
        total += parts[p, 32:72, :].astype(F32)
    total = total.astype(BF)
    y = place()
    i = lax.broadcasted_iota(jnp.int32, (256, 256), 0)
    j = lax.broadcasted_iota(jnp.int32, (256, 256), 1)
    place_of = ((i >> 1) & 7) * 32 + (i & 1) * 16 + (i >> 4)
    rows = jnp.concatenate([parts[p * 4 + y, 0:32, :] for p in range(8)], axis=0)
    rows = dot(jnp.where(j == place_of, 1.0, 0.0).astype(BF), rows).astype(BF)
    for z in range(16):
        out[z, 0:16, :] = rows[z * 16 : (z + 1) * 16, :]
        out[z, 16:56, :] = total


def layer_kernel(parts, out, four, sems):
    total = parts[0, 16:56, :].astype(F32)
    for p in range(1, 16):
        total += parts[p, 16:56, :].astype(F32)
    total = total.astype(BF)
    for p in range(4):
        four[p] = total
    copies = [pltpu.make_async_copy(four, out.at[p * 4 : p * 4 + 4], sems.at[p]) for p in range(8)]
    for copy in copies:
        copy.start()
    for copy in copies:
        copy.wait()


def logits_kernel(index, recv1, recv2, hidden, tiles, w1s, w1n, bias, w2s_t, w2n_t, out_t, ext, agg):
    far = jnp.concatenate([recv2[z, 0:16, :] for z in range(16)], axis=0)
    pre = dot(recv1[:, 0:128], w1s[...]) + dot(far, w1n[...]) + bias[...]
    i = lax.broadcasted_iota(jnp.int32, (128, 256), 0)
    live = dot(recv1[:, 256:384], jnp.where(i == 44, 1.0, 0.0).astype(BF))
    far = jnp.where(live > 0.5, jnp.maximum(pre, 0.0), 0.0).astype(BF)
    for b in range(4):
        ext[b] = hidden[b * 128 : (b + 1) * 128, :]
    for b in range(2):
        ext[4 + b] = far[b * 128 : (b + 1) * 128, :]
    for b in range(4):
        agg[b * 128 : (b + 1) * 128, :] = gather_tiles(index, tiles, ext, b)
    scores = dot_nt(w2s_t[...], hidden[...]) + dot_nt(w2n_t[...], agg[...])
    out_t[...] = scores.astype(BF)


def finish_kernel(total, self1, neigh1, bias, self2_t, neigh2_t):
    for h in range(2):
        cols = slice(h * 128, (h + 1) * 128)
        base = h * 640
        self1[:, cols] = total[base : base + 128, :].astype(F32)
        neigh1[:, cols] = total[base + 128 : base + 256, :].astype(F32)
        self2 = total[base + 256 : base + 432, :].astype(F32)
        self2_t[:, cols] = self2[0:172, :]
        bias[:, cols] = self2[172:173, :]
        neigh2_t[:, cols] = total[base + 432 : base + 608, :].astype(F32)[0:172, :]


def shape(dims, dtype):
    return jax.ShapeDtypeStruct(dims, dtype)


def before(rows, counts, *kept):
    here = [pltpu.with_memory_space_constraint(value, pltpu.HBM) for value in (rows, counts) + kept]
    return pl.pallas_call(
        before_kernel,
        out_shape=(shape((256, 384), BF), shape((256, 512), BF), shape((256, 512), BF), shape((256, 512), F32))
        + tuple(shape(value.shape, value.dtype) for value in kept),
        in_specs=[pl.BlockSpec(memory_space=pltpu.HBM)] * 11,
        out_specs=(VM,) * 13,
        scratch_shapes=[
            pltpu.VMEM((2, 128), jnp.int32),
            pltpu.VMEM((1, 128), jnp.int32),
            pltpu.SMEM((3, 1, 4), jnp.int32),
            pltpu.VMEM((6, 256, 128), F32),
            pltpu.VMEM((256, 512), BF),
            pltpu.SemaphoreType.DMA((12,)),
        ],
        compiler_params=PARAMS,
    )(*here)


def middle(index, recv, feat, tiles, pick, pick_out, own_t, grad_t, w1s, w1n, bias, w2s_t, w2n_t):
    return pl.pallas_call(
        middle_kernel,
        out_shape=(shape((512, 256), BF), shape((32, 72, 128), BF)),
        in_specs=[SM] + [VM] * 12,
        out_specs=(VM, VM),
        scratch_shapes=[
            pltpu.VMEM((6, 128, 128), BF),
            pltpu.VMEM((512, 256), BF),
            pltpu.VMEM((256, 512), BF),
            pltpu.VMEM((512, 256), BF),
        ],
        compiler_params=PARAMS,
    )(index, recv, feat, tiles, pick, pick_out, own_t, grad_t, w1s, w1n, bias, w2s_t, w2n_t)


def scores(index, recv1, recv2, hidden, tiles, w1s, w1n, bias, w2s_t, w2n_t):
    return pl.pallas_call(
        logits_kernel,
        out_shape=shape((172, 512), BF),
        in_specs=[SM] + [VM] * 9,
        out_specs=VM,
        scratch_shapes=[pltpu.VMEM((6, 128, 256), BF), pltpu.VMEM((512, 256), BF)],
        compiler_params=PARAMS,
    )(index, recv1, recv2, hidden, tiles, w1s, w1n, bias, w2s_t, w2n_t)


def after_plane(parts):
    return pl.pallas_call(
        plane_kernel,
        out_shape=shape((16, 56, 128), BF),
        in_specs=[VM],
        out_specs=VM,
        compiler_params=PARAMS,
    )(parts)


def after_layers(parts):
    return pl.pallas_call(
        layer_kernel,
        out_shape=shape((32, 40, 128), BF),
        in_specs=[VM],
        out_specs=pl.BlockSpec(memory_space=pltpu.HBM),
        scratch_shapes=[pltpu.VMEM((4, 40, 128), BF), pltpu.SemaphoreType.DMA((8,))],
        compiler_params=PARAMS,
    )(parts)


def finish(total):
    return pl.pallas_call(
        finish_kernel,
        out_shape=(
            shape((128, 256), F32),
            shape((128, 256), F32),
            shape((1, 256), F32),
            shape((172, 256), F32),
            shape((172, 256), F32),
        ),
        in_specs=[VM],
        out_specs=(VM,) * 5,
        compiler_params=PARAMS,
    )(total)


def exchange(values, axes):
    return lax.all_to_all(values, axes, split_axis=0, concat_axis=0, tiled=True)


def shards(
    features,
    send_rows,
    send_counts,
    tile_index,
    tile_weight,
    first_layer_self_weight,
    first_layer_neighbour_weight,
    layer1_bias,
    layer2_self,
    layer2_neigh,
    grad_logits,
):
    feat = features.reshape(512, 128)
    rows = jnp.swapaxes(send_rows.reshape(128, 2), 0, 1)
    counts = send_counts.reshape(1, 128)
    index = jnp.transpose(tile_index, (0, 3, 1, 2)).reshape(3, 1, 4)
    tiles = tile_weight.reshape(12, 128, 128)
    grad_t = jnp.swapaxes(grad_logits.reshape(512, 172), 0, 1)
    w2s_t = jnp.swapaxes(layer2_self, 0, 1)
    w2n_t = jnp.swapaxes(layer2_neigh, 0, 1)
    bias = layer1_bias.reshape(1, 256)

    send1, pick, pick_out, own_t, feat, grad_t, tiles, w1s, w1n, bias, w2s_t, w2n_t, index = before(
        rows, counts, feat, grad_t, tiles,
        first_layer_self_weight, first_layer_neighbour_weight, bias, w2s_t, w2n_t, index,
    )
    recv1 = exchange(send1.reshape(128, 2, 384), WIDE).reshape(256, 384)
    hidden, parts = middle(
        index, recv1, feat, tiles, pick, pick_out, own_t, grad_t,
        w1s, w1n, bias, w2s_t, w2n_t,
    )
    recv2 = exchange(after_plane(exchange(parts, PLANE)), "z")
    total = exchange(after_layers(recv2), PLANE)
    logits_t = scores(index, recv1, recv2, hidden, tiles, w1s, w1n, bias, w2s_t, w2n_t)
    self1, neigh1, bias1, self2_t, neigh2_t = finish(total.reshape(1280, 128))
    logits = jnp.swapaxes(logits_t, 0, 1).reshape(1, 1, 512, 172)
    return (
        logits,
        self1,
        neigh1,
        bias1.reshape(256),
        jnp.swapaxes(self2_t, 0, 1),
        jnp.swapaxes(neigh2_t, 0, 1),
    )


def solution(mesh):
    fine = Mesh(mesh.devices.reshape(16, 4, 2, 4), ("z", "x", "core", "y"))
    return jax.shard_map(
        shards,
        mesh=fine,
        in_specs=(
            P(WIDE, "y", None, None),
            P(WIDE, "y", None, None),
            P(WIDE, "y", None),
            P(WIDE, "y", None, None),
            P(WIDE, "y", None, None, None, None),
            P(),
            P(),
            P(),
            P(),
            P(),
            P(WIDE, "y", None, None),
        ),
        out_specs=(P(WIDE, "y", None, None), P(), P(), P(), P(), P()),
        check_vma=False,
    )
```

time: 106 us -> 99.4 us (0.938)
  blocking collectives: 81.2 us -> 73.1 us
  starting transfers between devices: 7.47 us -> 9.59 us
    all_to_all x3, blocking collectives: 81.2 us -> 73.1 us  [exchange(): return lax.all_to_all(values, axes, split_axis=0, concat_axis=0, tiled=True)]
    all_to_all x1, starting transfers between devices: 7.47 us -> 9.59 us  [exchange(): return lax.all_to_all(values, axes, split_axis=0, concat_axis=0, tiled=True)]
where the time goes in v5:
time: 99.4 us; the launch traced here: 99.1 us
  blocking collectives  73.1 us (74%)
  starting transfers between devices  9.59 us (10%)
  Pallas kernels  8.34 us (8%)
  waiting for transfers between devices  7.22 us (7%)
    all_to_all x3, blocking collectives, exchange(): return lax.all_to_all(values, axes, split_axis=0, concat_axis=0, tiled=True)  73.1 us
    all_to_all x1, starting transfers between devices, exchange(): return lax.all_to_all(values, axes, split_axis=0, concat_axis=0, tiled=True)  9.59 us
    all_to_all x1, waiting for transfers between devices, exchange(): return lax.all_to_all(values, axes, split_axis=0, concat_axis=0, tiled=True)  7.22 us
    pallas_call x1, Pallas kernels, middle(): pl.pallas_call(middle_kernel, out_shape=(shape((512, 256), BF), shape((32...  2.4 us
    pallas_call x1, Pallas kernels, scores(): pl.pallas_call(logits_kernel, out_shape=shape((172, 512), BF), in_specs=[...  2.23 us
  transfers between devices with their start and end apart: 1, of which 1 were waited for; matrix products, arithmetic and copies ran while one was open for 0% of the time, Pallas kernels for 2%

profile of v5, /device:TPU:1, one launch (start us, length us, event | category | flops | bytes accessed | tf_op | source)
XLA Modules:
  0.0 99.1 jit_solution(9189378919702653264)
XLA Ops:
  0.6 1.9 %shard_map.154 = (bf16[256,384]{1,0:T(8,128)(2,1)S(1)}, bf16[256,512]{1,0:T(8,128)(2,1)S(1)}, bf16[256,512]{1,0:T(8,128)(2,1)S(1)}, f32[256,512]{1,0:T(8,128)S(1...) custom-call(s32[2,128]{1,0:T(2,128)} %bitcast.30, ...), custom_call_target="tpu_custom_call" | custom-call | tf_op jit(solution)/shard_map/pallas_call | solution.py:204
  2.5 0.1 reshape.55
  2.6 38.2 %all_to_all.20 = bf16[128,2,384]{2,1,0:T(2,128)(2,1)S(1)} all-to-all(bf16[128,2,384]{2,1,0:T(2,128)(2,1)S(1)} %reshape.55), channel_id=1, replica_groups=mesh['z'=16,'x'=4,'core'=2,'y'=4] {'z','x','core'}, dimensions={0} | all-to-all | bytes 393216 | tf_op jit(solution)/shard_map/all_to_all | solution.py:287
  40.8 0.1 reshape.56.recv.recv1
  40.9 2.4 %shard_map.155 = (bf16[512,256]{1,0:T(8,128)(2,1)S(1)}, bf16[32,72,128]{2,1,0:T(8,128)(2,1)S(1)}) custom-call(s32[3,1,4]{2,1,0:T(1,128)S(1)} %get-tuple-element.26.index, bf16[256,384]{1,0:T(8,128)(2,1)S(1)} %reshape.56.recv.recv1, bf16[512,128]{1,0:T(8,128)(2,1)S(1)} %get-tuple-element.28.feat, bf16[12,128,128]{2,1,0:T(8,128)(2,1)S(1)} %get-tuple-element.29.tiles, ...), custom_call_target="tpu_custom_call" | custom-call | tf_op jit(solution)/shard_map/pallas_call | solution.py:223
  43.3 19.5 %all_to_all.21.parts = bf16[32,72,128]{2,1,0:T(8,128)(2,1)S(1)} all-to-all(bf16[32,72,128]{2,1,0:T(8,128)(2,1)S(1)} %get-tuple-element.39), channel_id=1, replica_groups=mesh['z'=16,'x'=4,'core'=2,'y'=4] {'x','core','y'}, dimensions={0} | all-to-all | bytes 1179648 | tf_op jit(solution)/shard_map/all_to_all | solution.py:287
  62.8 0.2 shard_map.156
  63.0 15.3 %all_to_all.22.recv2.parts = bf16[16,56,128]{2,1,0:T(8,128)(2,1)S(1)} all-to-all(bf16[16,56,128]{2,1,0:T(8,128)(2,1)S(1)} %shard_map.156), channel_id=1, replica_groups=mesh['z'=16,'x'=4,'core'=2,'y'=4] {'z'}, dimensions={0} | all-to-all | bytes 458752 | tf_op jit(solution)/shard_map/all_to_all | solution.py:287
  78.3 0.8 shard_map.158
  79.2 9.6 %all-to-all-start.3 = ((bf16[32,40,128]{2,1,0:T(8,128)(2,1)}), bf16[32,40,128]{2,1,0:T(8,128)(2,1)S(1)}, u32[]{:S(2)}, u32[]{:S(2)}) async-start(bf16[32,40,128]{2,1,0:T(8,128)(2,1)} %shard_map.158), calls=%async_computation.3 | async-start | bytes 655360 | tf_op jit(solution)/shard_map/all_to_all | solution.py:287
  88.8 2.2 %shard_map.157 = bf16[172,512]{1,0:T(8,128)(2,1)} custom-call(s32[3,1,4]{2,1,0:T(1,128)S(1)} %get-tuple-element.26.index, bf16[256,384]{1,0:T(8,128)(2,1)S(1)} %reshape.56.recv.recv1, bf16[16,56,128]{2,1,0:T(8,128)(2,1)S(1)} %all_to_all.22.recv2.parts, bf16[512,256]{1,0:T(8,128)(2,1)S(1)} %get-tuple-element.40.hidden, ...), custom_call_target="tpu_custom_call" | custom-call | tf_op jit(solution)/shard_map/pallas_call | solution.py:239
  91.0 7.2 %all-to-all-done.3 = bf16[32,40,128]{2,1,0:T(8,128)(2,1)S(1)} async-done(((bf16[32,40,128]{2,1,0:T(8,128)(2,1)}), bf16[32,40,128]{2,1,0:T(8,128)(2,1)S(1)}, u32[]{:S(2)}, u32[]{:S(2)}) %all-to-all-start.3) | async-done | bytes 327712 | tf_op jit(solution)/shard_map/all_to_all | solution.py:287
  98.2 0.8 shard_map.159
Async XLA Ops:
  79.2 19.1 %all-to-all-start.3 = ((bf16[32,40,128]{2,1,0:T(8,128)(2,1)}), bf16[32,40,128]{2,1,0:T(8,128)(2,1)S(1)}, u32[]{:S(2)}, u32[]{:S(2)}) async-start(bf16[32,40,128]{2,1,0:T(8,128)(2,1)} %shard_map.158), calls=%async_computation.3 | async-start | bytes 655360 | tf_op jit(solution)/shard_map/all_to_all | solution.py:287

commit v6 on v5

--- a/solution.py
+++ b/solution.py
@@ -22,9 +22,8 @@
     return lax.dot_general(a, b, (((1,), (1,)), ((), ())), preferred_element_type=F32)
 
 
-def split(values):
-    upper = values.astype(BF)
-    return upper, (values - upper.astype(F32)).astype(BF)
+def dot_tn(a, b):
+    return lax.dot_general(a, b, (((0,), (0,)), ((), ())), preferred_element_type=F32)
 
 
 def place():
@@ -118,16 +117,14 @@
     wide_w[256 : 256 + 172, :] = w2n_t[...]
     returned_t = recv[:, 128:384].astype(F32).T.astype(BF)
     back_t = own_t[...] + dot(returned_t, pick[...])
-    upper_t, lower_t = split(back_t)
-    upper, lower = split(back_t.T)
+    upper_t = back_t.astype(BF)
     grad = padded[...]
-    grad_hidden = dot(grad.astype(F32).T.astype(BF), wide_w[0:256, :])
-    grad_hidden += dot(upper, wide_w[256:512, :]) + dot(lower, wide_w[256:512, :])
+    grad_hidden = dot_tn(jnp.concatenate([grad, upper_t], axis=0), wide_w[...])
     grad_pre = jnp.where(pre > 0, grad_hidden, 0.0).astype(BF)
     first = dot(both[...].astype(F32).T.astype(BF), grad_pre)
     bias_sum = jnp.sum(grad_pre.astype(F32), axis=0, keepdims=True)
     self2 = dot(grad, hid)
-    neigh2 = dot(upper_t, hid) + dot(lower_t, hid)
+    neigh2 = dot(upper_t, hid)
     row = lax.broadcasted_iota(jnp.int32, (176, 256), 0)
     self2 = jnp.where(row == 172, bias_sum, self2[0:176, :])
     neigh2 = neigh2[0:176, :]

time: 99.4 us -> 98.7 us (level)
  no operation moved by 1% of the time
where the time goes in v6:
time: 98.7 us; the launch traced here: 98.4 us
  blocking collectives  73.1 us (74%)
  starting transfers between devices  9.59 us (10%)
  Pallas kernels  7.72 us (8%)
  waiting for transfers between devices  7.23 us (7%)
    all_to_all x3, blocking collectives, exchange(): return lax.all_to_all(values, axes, split_axis=0, concat_axis=0, tiled=True)  73.1 us
    all_to_all x1, starting transfers between devices, exchange(): return lax.all_to_all(values, axes, split_axis=0, concat_axis=0, tiled=True)  9.59 us
    all_to_all x1, waiting for transfers between devices, exchange(): return lax.all_to_all(values, axes, split_axis=0, concat_axis=0, tiled=True)  7.23 us
    pallas_call x1, Pallas kernels, scores(): pl.pallas_call(logits_kernel, out_shape=shape((172, 512), BF), in_specs=[...  2.23 us
  transfers between devices with their start and end apart: 1, of which 1 were waited for; matrix products, arithmetic and copies ran while one was open for 0% of the time, Pallas kernels for 2%

profile of v6, /device:TPU:1, one launch (start us, length us, event | category | flops | bytes accessed | tf_op | source)
XLA Modules:
  0.0 98.4 jit_solution(7537639368608872721)
XLA Ops:
  0.6 1.9 %shard_map.154 = (bf16[256,384]{1,0:T(8,128)(2,1)S(1)}, bf16[256,512]{1,0:T(8,128)(2,1)S(1)}, bf16[256,512]{1,0:T(8,128)(2,1)S(1)}, f32[256,512]{1,0:T(8,128)S(1...) custom-call(s32[2,128]{1,0:T(2,128)} %bitcast.30, ...), custom_call_target="tpu_custom_call" | custom-call | tf_op jit(solution)/shard_map/pallas_call | solution.py:201
  2.5 0.1 reshape.55
  2.6 38.2 %all_to_all.20 = bf16[128,2,384]{2,1,0:T(2,128)(2,1)S(1)} all-to-all(bf16[128,2,384]{2,1,0:T(2,128)(2,1)S(1)} %reshape.55), channel_id=1, replica_groups=mesh['z'=16,'x'=4,'core'=2,'y'=4] {'z','x','core'}, dimensions={0} | all-to-all | bytes 393216 | tf_op jit(solution)/shard_map/all_to_all | solution.py:284
  40.8 0.1 reshape.56.recv.recv1
  40.9 1.8 %shard_map.155 = (bf16[512,256]{1,0:T(8,128)(2,1)S(1)}, bf16[32,72,128]{2,1,0:T(8,128)(2,1)S(1)}) custom-call(s32[3,1,4]{2,1,0:T(1,128)S(1)} %get-tuple-element.26.index, bf16[256,384]{1,0:T(8,128)(2,1)S(1)} %reshape.56.recv.recv1, bf16[512,128]{1,0:T(8,128)(2,1)S(1)} %get-tuple-element.28.feat, bf16[12,128,128]{2,1,0:T(8,128)(2,1)S(1)} %get-tuple-element.29.tiles, ...), custom_call_target="tpu_custom_call" | custom-call | tf_op jit(solution)/shard_map/pallas_call | solution.py:220
  42.7 19.5 %all_to_all.21.parts = bf16[32,72,128]{2,1,0:T(8,128)(2,1)S(1)} all-to-all(bf16[32,72,128]{2,1,0:T(8,128)(2,1)S(1)} %get-tuple-element.39), channel_id=1, replica_groups=mesh['z'=16,'x'=4,'core'=2,'y'=4] {'x','core','y'}, dimensions={0} | all-to-all | bytes 1179648 | tf_op jit(solution)/shard_map/all_to_all | solution.py:284
  62.2 0.2 shard_map.156
  62.4 15.3 %all_to_all.22.recv2.parts = bf16[16,56,128]{2,1,0:T(8,128)(2,1)S(1)} all-to-all(bf16[16,56,128]{2,1,0:T(8,128)(2,1)S(1)} %shard_map.156), channel_id=1, replica_groups=mesh['z'=16,'x'=4,'core'=2,'y'=4] {'z'}, dimensions={0} | all-to-all | bytes 458752 | tf_op jit(solution)/shard_map/all_to_all | solution.py:284
  77.7 0.8 shard_map.158
  78.5 9.6 %all-to-all-start.3 = ((bf16[32,40,128]{2,1,0:T(8,128)(2,1)}), bf16[32,40,128]{2,1,0:T(8,128)(2,1)S(1)}, u32[]{:S(2)}, u32[]{:S(2)}) async-start(bf16[32,40,128]{2,1,0:T(8,128)(2,1)} %shard_map.158), calls=%async_computation.3 | async-start | bytes 655360 | tf_op jit(solution)/shard_map/all_to_all | solution.py:284
  88.1 2.2 %shard_map.157 = bf16[172,512]{1,0:T(8,128)(2,1)} custom-call(s32[3,1,4]{2,1,0:T(1,128)S(1)} %get-tuple-element.26.index, bf16[256,384]{1,0:T(8,128)(2,1)S(1)} %reshape.56.recv.recv1, bf16[16,56,128]{2,1,0:T(8,128)(2,1)S(1)} %all_to_all.22.recv2.parts, bf16[512,256]{1,0:T(8,128)(2,1)S(1)} %get-tuple-element.40.hidden, ...), custom_call_target="tpu_custom_call" | custom-call | tf_op jit(solution)/shard_map/pallas_call | solution.py:236
  90.4 7.2 %all-to-all-done.3 = bf16[32,40,128]{2,1,0:T(8,128)(2,1)S(1)} async-done(((bf16[32,40,128]{2,1,0:T(8,128)(2,1)}), bf16[32,40,128]{2,1,0:T(8,128)(2,1)S(1)}, u32[]{:S(2)}, u32[]{:S(2)}) %all-to-all-start.3) | async-done | bytes 327712 | tf_op jit(solution)/shard_map/all_to_all | solution.py:284
  97.6 0.8 shard_map.159
Async XLA Ops:
  78.5 19.1 %all-to-all-start.3 = ((bf16[32,40,128]{2,1,0:T(8,128)(2,1)}), bf16[32,40,128]{2,1,0:T(8,128)(2,1)S(1)}, u32[]{:S(2)}, u32[]{:S(2)}) async-start(bf16[32,40,128]{2,1,0:T(8,128)(2,1)} %shard_map.158), calls=%async_computation.3 | async-start | bytes 655360 | tf_op jit(solution)/shard_map/all_to_all | solution.py:284

commit v7 on v6

--- a/solution.py
+++ b/solution.py
@@ -93,15 +93,27 @@
 
 
 def middle_kernel(
-    index, recv, feat, tiles, pick, pick_out, own_t, grad_t, w1s, w1n, bias, w2s_t, w2n_t,
-    hidden, out, ext, both, padded, wide_w,
+    index_in, recv, feat, tiles, pick, pick_out, own_t, grad_t, w1s, w1n, bias, w2s_t, w2n_t,
+    hidden, out, ext, both, padded, wide_w, index, sem,
 ):
+    copy = pltpu.make_async_copy(index_in, index, sem)
+    copy.start()
     for b in range(4):
         ext[b] = feat[b * 128 : (b + 1) * 128, :]
     for b in range(2):
         ext[4 + b] = recv[b * 128 : (b + 1) * 128, 0:128]
     both[:, 0:128] = feat[...]
     wide_w[...] = jnp.zeros_like(wide_w)
+    padded[...] = jnp.zeros_like(padded)
+    padded[0:172, :] = grad_t[...]
+    wide_w[0:172, :] = w2s_t[...]
+    wide_w[256 : 256 + 172, :] = w2n_t[...]
+    returned_t = recv[:, 128:384].astype(F32).T.astype(BF)
+    back_t = own_t[...] + dot(returned_t, pick[...])
+    copy.wait()
+    upper_t = back_t.astype(BF)
+    grad = padded[...]
+    grad_hidden = dot_tn(jnp.concatenate([grad, upper_t], axis=0), wide_w[...])
     for b in range(4):
         both[b * 128 : (b + 1) * 128, 128:256] = gather_tiles(index, tiles, ext, b)
     picked = dot(pick_out[...], both[:, 128:256]).astype(BF)
@@ -111,15 +123,6 @@
     pre = dot(both[:, 0:128], w1s[...]) + dot(both[:, 128:256], w1n[...]) + bias[...]
     hid = jnp.maximum(pre, 0.0).astype(BF)
     hidden[...] = hid
-    padded[...] = jnp.zeros_like(padded)
-    padded[0:172, :] = grad_t[...]
-    wide_w[0:172, :] = w2s_t[...]
-    wide_w[256 : 256 + 172, :] = w2n_t[...]
-    returned_t = recv[:, 128:384].astype(F32).T.astype(BF)
-    back_t = own_t[...] + dot(returned_t, pick[...])
-    upper_t = back_t.astype(BF)
-    grad = padded[...]
-    grad_hidden = dot_tn(jnp.concatenate([grad, upper_t], axis=0), wide_w[...])
     grad_pre = jnp.where(pre > 0, grad_hidden, 0.0).astype(BF)
     first = dot(both[...].astype(F32).T.astype(BF), grad_pre)
     bias_sum = jnp.sum(grad_pre.astype(F32), axis=0, keepdims=True)
@@ -150,21 +153,43 @@
         out[z, 16:56, :] = total
 
 
-def layer_kernel(parts, out, four, sems):
+def layer_kernel(parts, out):
     total = parts[0, 16:56, :].astype(F32)
     for p in range(1, 16):
         total += parts[p, 16:56, :].astype(F32)
     total = total.astype(BF)
-    for p in range(4):
-        four[p] = total
-    copies = [pltpu.make_async_copy(four, out.at[p * 4 : p * 4 + 4], sems.at[p]) for p in range(8)]
-    for copy in copies:
-        copy.start()
-    for copy in copies:
-        copy.wait()
-
-
-def logits_kernel(index, recv1, recv2, hidden, tiles, w1s, w1n, bias, w2s_t, w2n_t, out_t, ext, agg):
+    for p in range(32):
+        out[p] = total
+
+
+def last_kernel(
+    index_in, total, recv1, recv2, hidden, tiles, w1s, w1n, bias, w2s_t, w2n_t,
+    logits_out, self1_out, neigh1_out, bias_out, self2_out, neigh2_out,
+    logits, self1, neigh1, bias1, self2_t, neigh2_t, ext, agg, sems, index, index_sem,
+):
+    copies = []
+    fetch = pltpu.make_async_copy(index_in, index, index_sem)
+    fetch.start()
+
+    def leave(value, target):
+        copies.append(pltpu.make_async_copy(value, target, sems.at[len(copies)]))
+        copies[-1].start()
+
+    def both(first, rows):
+        halves = [total[base + first : base + first + rows, :].astype(F32) for base in (0, 640)]
+        return jnp.concatenate(halves, axis=1)
+
+    self1[...] = both(0, 128)
+    leave(self1, self1_out)
+    neigh1[...] = both(128, 128)
+    leave(neigh1, neigh1_out)
+    value = both(256, 176)
+    self2_t[...] = value[0:172, :]
+    leave(self2_t, self2_out)
+    bias1[...] = value[172:173, :]
+    leave(bias1, bias_out)
+    neigh2_t[...] = both(432, 176)[0:172, :]
+    leave(neigh2_t, neigh2_out)
     far = jnp.concatenate([recv2[z, 0:16, :] for z in range(16)], axis=0)
     pre = dot(recv1[:, 0:128], w1s[...]) + dot(far, w1n[...]) + bias[...]
     i = lax.broadcasted_iota(jnp.int32, (128, 256), 0)
@@ -174,22 +199,15 @@
         ext[b] = hidden[b * 128 : (b + 1) * 128, :]
     for b in range(2):
         ext[4 + b] = far[b * 128 : (b + 1) * 128, :]
+    scores = dot_nt(w2s_t[...], hidden[...])
+    fetch.wait()
     for b in range(4):
         agg[b * 128 : (b + 1) * 128, :] = gather_tiles(index, tiles, ext, b)
-    scores = dot_nt(w2s_t[...], hidden[...]) + dot_nt(w2n_t[...], agg[...])
-    out_t[...] = scores.astype(BF)
-
-
-def finish_kernel(total, self1, neigh1, bias, self2_t, neigh2_t):
-    for h in range(2):
-        cols = slice(h * 128, (h + 1) * 128)
-        base = h * 640
-        self1[:, cols] = total[base : base + 128, :].astype(F32)
-        neigh1[:, cols] = total[base + 128 : base + 256, :].astype(F32)
-        self2 = total[base + 256 : base + 432, :].astype(F32)
-        self2_t[:, cols] = self2[0:172, :]
-        bias[:, cols] = self2[172:173, :]
-        neigh2_t[:, cols] = total[base + 432 : base + 608, :].astype(F32)[0:172, :]
+    scores += dot_nt(w2n_t[...], agg[...])
+    logits[...] = scores.astype(BF)
+    leave(logits, logits_out)
+    for copy in copies:
+        copy.wait()
 
 
 def shape(dims, dtype):
@@ -220,27 +238,18 @@
     return pl.pallas_call(
         middle_kernel,
         out_shape=(shape((512, 256), BF), shape((32, 72, 128), BF)),
-        in_specs=[SM] + [VM] * 12,
+        in_specs=[VM] * 13,
         out_specs=(VM, VM),
         scratch_shapes=[
             pltpu.VMEM((6, 128, 128), BF),
             pltpu.VMEM((512, 256), BF),
             pltpu.VMEM((256, 512), BF),
             pltpu.VMEM((512, 256), BF),
+            pltpu.SMEM((3, 1, 4), jnp.int32),
+            pltpu.SemaphoreType.DMA,
         ],
         compiler_params=PARAMS,
     )(index, recv, feat, tiles, pick, pick_out, own_t, grad_t, w1s, w1n, bias, w2s_t, w2n_t)
-
-
-def scores(index, recv1, recv2, hidden, tiles, w1s, w1n, bias, w2s_t, w2n_t):
-    return pl.pallas_call(
-        logits_kernel,
-        out_shape=shape((172, 512), BF),
-        in_specs=[SM] + [VM] * 9,
-        out_specs=VM,
-        scratch_shapes=[pltpu.VMEM((6, 128, 256), BF), pltpu.VMEM((512, 256), BF)],
-        compiler_params=PARAMS,
-    )(index, recv1, recv2, hidden, tiles, w1s, w1n, bias, w2s_t, w2n_t)
 
 
 def after_plane(parts):
@@ -258,26 +267,29 @@
         layer_kernel,
         out_shape=shape((32, 40, 128), BF),
         in_specs=[VM],
-        out_specs=pl.BlockSpec(memory_space=pltpu.HBM),
-        scratch_shapes=[pltpu.VMEM((4, 40, 128), BF), pltpu.SemaphoreType.DMA((8,))],
+        out_specs=VM,
         compiler_params=PARAMS,
     )(parts)
 
 
-def finish(total):
-    return pl.pallas_call(
-        finish_kernel,
-        out_shape=(
-            shape((128, 256), F32),
-            shape((128, 256), F32),
-            shape((1, 256), F32),
-            shape((172, 256), F32),
-            shape((172, 256), F32),
-        ),
-        in_specs=[VM],
-        out_specs=(VM,) * 5,
-        compiler_params=PARAMS,
-    )(total)
+def last(index, total, recv1, recv2, hidden, tiles, w1s, w1n, bias, w2s_t, w2n_t):
+    shapes = (
+        shape((172, 512), BF),
+        shape((128, 256), F32),
+        shape((128, 256), F32),
+        shape((1, 256), F32),
+        shape((172, 256), F32),
+        shape((172, 256), F32),
+    )
+    return pl.pallas_call(
+        last_kernel,
+        out_shape=shapes,
+        in_specs=[VM] * 11,
+        out_specs=(pl.BlockSpec(memory_space=pltpu.HBM),) * 6,
+        scratch_shapes=[pltpu.VMEM(one.shape, one.dtype) for one in shapes]
+        + [pltpu.VMEM((6, 128, 256), BF), pltpu.VMEM((512, 256), BF), pltpu.SemaphoreType.DMA((6,)), pltpu.SMEM((3, 1, 4), jnp.int32), pltpu.SemaphoreType.DMA],
+        compiler_params=PARAMS,
+    )(index, total, recv1, recv2, hidden, tiles, w1s, w1n, bias, w2s_t, w2n_t)
 
 
 def exchange(values, axes):
@@ -318,8 +330,9 @@
     )
     recv2 = exchange(after_plane(exchange(parts, PLANE)), "z")
     total = exchange(after_layers(recv2), PLANE)
-    logits_t = scores(index, recv1, recv2, hidden, tiles, w1s, w1n, bias, w2s_t, w2n_t)
-    self1, neigh1, bias1, self2_t, neigh2_t = finish(total.reshape(1280, 128))
+    logits_t, self1, neigh1, bias1, self2_t, neigh2_t = last(
+        index, total.reshape(1280, 128), recv1, recv2, hidden, tiles, w1s, w1n, bias, w2s_t, w2n_t,
+    )
     logits = jnp.swapaxes(logits_t, 0, 1).reshape(1, 1, 512, 172)
     return (
         logits,

time: 98.7 us -> 98.7 us (level)
  blocking collectives: 73.1 us -> 91.9 us
  starting transfers between devices: 9.59 us -> 0 us
  waiting for transfers between devices: 7.23 us -> 0 us
  Pallas kernels: 7.72 us -> 5.75 us
    all_to_all x3 -> x4, blocking collectives: 73.1 us -> 91.9 us  [exchange(): return lax.all_to_all(values, axes, split_axis=0, concat_axis=0, tiled=True)]
    all_to_all x1 -> x0, starting transfers between devices: 9.59 us -> none  [exchange(): return lax.all_to_all(values, axes, split_axis=0, concat_axis=0, tiled=True)]
    all_to_all x1 -> x0, waiting for transfers between devices: 7.23 us -> none  [exchange(): return lax.all_to_all(values, axes, split_axis=0, concat_axis=0, tiled=True)]
    pallas_call x2 -> x1, Pallas kernels: 3.07 us -> 2 us  [last(): pl.pallas_call(last_kernel, out_shape=shapes, in_specs=[VM] * 11, out_spe...]
  transfers between devices with their start and end apart: 1 -> 0, of which waited for: 1 -> 0; matrix products, arithmetic and copies ran while one was open for 0% -> 0% of each run, Pallas kernels for 2% -> 0%
where the time goes in v7:
time: 98.7 us; the launch traced here: 98.5 us
  blocking collectives  91.9 us (93%)
  Pallas kernels  5.75 us (6%)
    all_to_all x4, blocking collectives, exchange(): return lax.all_to_all(values, axes, split_axis=0, concat_axis=0, tiled=True)  91.9 us
    pallas_call x1, Pallas kernels, last(): pl.pallas_call(last_kernel, out_shape=shapes, in_specs=[VM] * 11, out_spe...  2 us

profile of v7, /device:TPU:1, one launch (start us, length us, event | category | flops | bytes accessed | tf_op | source)
XLA Modules:
  0.0 98.5 jit_solution(10919287597629311391)
XLA Ops:
  0.6 1.9 %shard_map.154 = (bf16[256,384]{1,0:T(8,128)(2,1)S(1)}, bf16[256,512]{1,0:T(8,128)(2,1)S(1)}, bf16[256,512]{1,0:T(8,128)(2,1)S(1)}, f32[256,512]{1,0:T(8,128)S(1...) custom-call(s32[2,128]{1,0:T(2,128)} %bitcast.29, ...), custom_call_target="tpu_custom_call" | custom-call | tf_op jit(solution)/shard_map/pallas_call | solution.py:219
  2.5 0.1 reshape.55
  2.6 38.2 %all_to_all.20 = bf16[128,2,384]{2,1,0:T(2,128)(2,1)S(1)} all-to-all(bf16[128,2,384]{2,1,0:T(2,128)(2,1)S(1)} %reshape.55), channel_id=1, replica_groups=mesh['z'=16,'x'=4,'core'=2,'y'=4] {'z','x','core'}, dimensions={0} | all-to-all | bytes 393216 | tf_op jit(solution)/shard_map/all_to_all | solution.py:296
  40.8 0.1 reshape.56.recv.recv1
  40.9 1.7 %shard_map.155 = (bf16[512,256]{1,0:T(8,128)(2,1)S(1)}, bf16[32,72,128]{2,1,0:T(8,128)(2,1)S(1)}) custom-call(s32[3,1,4]{2,1,0:T(1,128)S(1)} %get-tuple-element.27.index_in, bf16[256,384]{1,0:T(8,128)(2,1)S(1)} %reshape.56.recv.recv1, bf16[512,128]{1,0:T(8,128)(2,1)S(1)} %get-tuple-element.29.feat, bf16[12,128,128]{2,1,0:T(8,128)(2,1)S(1)} %get-tuple-element.30.tiles, ...), custom_call_target="tpu_custom_call" | custom-call | tf_op jit(solution)/shard_map/pallas_call | solution.py:238
  42.6 19.5 %all_to_all.21.parts = bf16[32,72,128]{2,1,0:T(8,128)(2,1)S(1)} all-to-all(bf16[32,72,128]{2,1,0:T(8,128)(2,1)S(1)} %get-tuple-element.40), channel_id=1, replica_groups=mesh['z'=16,'x'=4,'core'=2,'y'=4] {'x','core','y'}, dimensions={0} | all-to-all | bytes 1179648 | tf_op jit(solution)/shard_map/all_to_all | solution.py:296
  62.1 0.2 shard_map.156
  62.3 15.3 %all_to_all.22.parts.recv2 = bf16[16,56,128]{2,1,0:T(8,128)(2,1)S(1)} all-to-all(bf16[16,56,128]{2,1,0:T(8,128)(2,1)S(1)} %shard_map.156), channel_id=1, replica_groups=mesh['z'=16,'x'=4,'core'=2,'y'=4] {'z'}, dimensions={0} | all-to-all | bytes 458752 | tf_op jit(solution)/shard_map/all_to_all | solution.py:296
  77.6 18.8 %all_to_all.23 = bf16[32,40,128]{2,1,0:T(8,128)(2,1)S(1)} all-to-all(bf16[32,40,128]{2,1,0:T(8,128)(2,1)S(1)} %shard_map.157), channel_id=1, replica_groups=mesh['z'=16,'x'=4,'core'=2,'y'=4] {'x','core','y'}, dimensions={0} | all-to-all | bytes 655360 | tf_op jit(solution)/shard_map/all_to_all | solution.py:296
  96.5 2.0 %shard_map.158 = (bf16[172,512]{1,0:T(8,128)(2,1)}, f32[128,256]{1,0:T(8,128)}, f32[128,256]{1,0:T(8,128)}, f32[1,256]{1,0:T(1,128)}, f32[172,256]{1,0:T(8,128)}, /*index=5*/f32[172,256]{1,0:T(8,128)}) custom-call(s32[3,1,4]{2,1,0:T(1,128)S(1)} %get-tuple-element.27.index_in, bf16[1280,128]{1,0:T(8,128)(2,1)S(1)} %bitcast.22, ...), custom_call_target="tpu_custom_call" | custom-call | tf_op jit(solution)/shard_map/pallas_call | solution.py:284
  (1 shorter events, 0.0 us)

commit v8 on v7

--- a/solution.py
+++ b/solution.py
@@ -98,6 +98,7 @@
 ):
     copy = pltpu.make_async_copy(index_in, index, sem)
     copy.start()
+    recv = recv[...].reshape(256, 384)
     for b in range(4):
         ext[b] = feat[b * 128 : (b + 1) * 128, :]
     for b in range(2):
@@ -170,6 +171,7 @@
     copies = []
     fetch = pltpu.make_async_copy(index_in, index, index_sem)
     fetch.start()
+    recv1 = recv1[...].reshape(256, 384)
 
     def leave(value, target):
         copies.append(pltpu.make_async_copy(value, target, sems.at[len(copies)]))
@@ -180,16 +182,11 @@
         return jnp.concatenate(halves, axis=1)
 
     self1[...] = both(0, 128)
-    leave(self1, self1_out)
     neigh1[...] = both(128, 128)
-    leave(neigh1, neigh1_out)
     value = both(256, 176)
     self2_t[...] = value[0:172, :]
-    leave(self2_t, self2_out)
     bias1[...] = value[172:173, :]
-    leave(bias1, bias_out)
     neigh2_t[...] = both(432, 176)[0:172, :]
-    leave(neigh2_t, neigh2_out)
     far = jnp.concatenate([recv2[z, 0:16, :] for z in range(16)], axis=0)
     pre = dot(recv1[:, 0:128], w1s[...]) + dot(far, w1n[...]) + bias[...]
     i = lax.broadcasted_iota(jnp.int32, (128, 256), 0)
@@ -201,6 +198,11 @@
         ext[4 + b] = far[b * 128 : (b + 1) * 128, :]
     scores = dot_nt(w2s_t[...], hidden[...])
     fetch.wait()
+    leave(self1, self1_out)
+    leave(neigh1, neigh1_out)
+    leave(self2_t, self2_out)
+    leave(bias1, bias_out)
+    leave(neigh2_t, neigh2_out)
     for b in range(4):
         agg[b * 128 : (b + 1) * 128, :] = gather_tiles(index, tiles, ext, b)
     scores += dot_nt(w2n_t[...], agg[...])
@@ -323,7 +325,7 @@
         rows, counts, feat, grad_t, tiles,
         first_layer_self_weight, first_layer_neighbour_weight, bias, w2s_t, w2n_t, index,
     )
-    recv1 = exchange(send1.reshape(128, 2, 384), WIDE).reshape(256, 384)
+    recv1 = exchange(send1.reshape(128, 2, 384), WIDE)
     hidden, parts = middle(
         index, recv1, feat, tiles, pick, pick_out, own_t, grad_t,
         w1s, w1n, bias, w2s_t, w2n_t,

time: 98.7 us -> 98.7 us (level)
  no operation moved by 1% of the time
where the time goes in v8:
time: 98.7 us; the launch traced here: 98.4 us
  blocking collectives  91.9 us (93%)
  Pallas kernels  5.74 us (6%)
    all_to_all x4, blocking collectives, exchange(): return lax.all_to_all(values, axes, split_axis=0, concat_axis=0, tiled=True)  91.9 us
    pallas_call x1, Pallas kernels, last(): pl.pallas_call(last_kernel, out_shape=shapes, in_specs=[VM] * 11, out_spe...  1.99 us

profile of v8, /device:TPU:1, one launch (start us, length us, event | category | flops | bytes accessed | tf_op | source)
XLA Modules:
  0.0 98.4 jit_solution(2632618738683734045)
XLA Ops:
  0.6 1.9 %shard_map.154 = (bf16[256,384]{1,0:T(8,128)(2,1)S(1)}, bf16[256,512]{1,0:T(8,128)(2,1)S(1)}, bf16[256,512]{1,0:T(8,128)(2,1)S(1)}, f32[256,512]{1,0:T(8,128)S(1...) custom-call(s32[2,128]{1,0:T(2,128)} %bitcast.29, ...), custom_call_target="tpu_custom_call" | custom-call | tf_op jit(solution)/shard_map/pallas_call | solution.py:221
  2.5 0.1 reshape.52
  2.6 38.2 %all_to_all.20.recv.recv1 = bf16[128,2,384]{2,1,0:T(2,128)(2,1)S(1)} all-to-all(bf16[128,2,384]{2,1,0:T(2,128)(2,1)S(1)} %reshape.52), channel_id=1, replica_groups=mesh['z'=16,'x'=4,'core'=2,'y'=4] {'z','x','core'}, dimensions={0} | all-to-all | bytes 393216 | tf_op jit(solution)/shard_map/all_to_all | solution.py:298
  40.8 1.7 %shard_map.155 = (bf16[512,256]{1,0:T(8,128)(2,1)S(1)}, bf16[32,72,128]{2,1,0:T(8,128)(2,1)S(1)}) custom-call(s32[3,1,4]{2,1,0:T(1,128)S(1)} %get-tuple-element.27.index_in, bf16[128,2,384]{2,1,0:T(2,128)(2,1)S(1)} %all_to_all.20.recv.recv1, bf16[512,128]{1,0:T(8,128)(2,1)S(1)} %get-tuple-element.29.feat, bf16[12,128,128]{2,1,0:T(8,128)(2,1)S(1)} %get-tuple-element.30.tiles, ...), custom_call_target="tpu_custom_call" | custom-call | tf_op jit(solution)/shard_map/pallas_call | solution.py:240
  42.5 19.5 %all_to_all.21.parts = bf16[32,72,128]{2,1,0:T(8,128)(2,1)S(1)} all-to-all(bf16[32,72,128]{2,1,0:T(8,128)(2,1)S(1)} %get-tuple-element.40), channel_id=1, replica_groups=mesh['z'=16,'x'=4,'core'=2,'y'=4] {'x','core','y'}, dimensions={0} | all-to-all | bytes 1179648 | tf_op jit(solution)/shard_map/all_to_all | solution.py:298
  62.0 0.2 shard_map.156
  62.2 15.3 %all_to_all.22.parts.recv2 = bf16[16,56,128]{2,1,0:T(8,128)(2,1)S(1)} all-to-all(bf16[16,56,128]{2,1,0:T(8,128)(2,1)S(1)} %shard_map.156), channel_id=1, replica_groups=mesh['z'=16,'x'=4,'core'=2,'y'=4] {'z'}, dimensions={0} | all-to-all | bytes 458752 | tf_op jit(solution)/shard_map/all_to_all | solution.py:298
  77.6 18.8 %all_to_all.23 = bf16[32,40,128]{2,1,0:T(8,128)(2,1)S(1)} all-to-all(bf16[32,40,128]{2,1,0:T(8,128)(2,1)S(1)} %shard_map.157), channel_id=1, replica_groups=mesh['z'=16,'x'=4,'core'=2,'y'=4] {'x','core','y'}, dimensions={0} | all-to-all | bytes 655360 | tf_op jit(solution)/shard_map/all_to_all | solution.py:298
  96.4 2.0 %shard_map.158 = (bf16[172,512]{1,0:T(8,128)(2,1)}, f32[128,256]{1,0:T(8,128)}, f32[128,256]{1,0:T(8,128)}, f32[1,256]{1,0:T(1,128)}, f32[172,256]{1,0:T(8,128)}, /*index=5*/f32[172,256]{1,0:T(8,128)}) custom-call(s32[3,1,4]{2,1,0:T(1,128)S(1)} %get-tuple-element.27.index_in, bf16[1280,128]{1,0:T(8,128)(2,1)S(1)} %bitcast.22, ...), custom_call_target="tpu_custom_call" | custom-call | tf_op jit(solution)/shard_map/pallas_call | solution.py:286
  (1 shorter events, 0.0 us)

commit v9 on v7

--- a/solution.py
+++ b/solution.py
@@ -86,7 +86,7 @@
 
 
 def gather_tiles(index, tiles, ext, b):
-    total = dot(tiles[b * 3], ext[index[0, 0, b]])
+    total = dot(tiles[b * 3], ext[b])
     total += dot(tiles[b * 3 + 1], ext[index[1, 0, b]])
     total += dot(tiles[b * 3 + 2], ext[index[2, 0, b]])
     return total.astype(BF)

time: 98.7 us -> 98.7 us (level)
  no operation moved by 1% of the time
where the time goes in v9:
time: 98.7 us; the launch traced here: 98.5 us
  blocking collectives  91.9 us (93%)
  Pallas kernels  5.75 us (6%)
    all_to_all x4, blocking collectives, exchange(): return lax.all_to_all(values, axes, split_axis=0, concat_axis=0, tiled=True)  91.9 us
    pallas_call x1, Pallas kernels, last(): pl.pallas_call(last_kernel, out_shape=shapes, in_specs=[VM] * 11, out_spe...  2 us

profile of v9, /device:TPU:1, one launch (start us, length us, event | category | flops | bytes accessed | tf_op | source)
XLA Modules:
  0.0 98.5 jit_solution(10256265748558103178)
XLA Ops:
  0.6 1.9 %shard_map.154 = (bf16[256,384]{1,0:T(8,128)(2,1)S(1)}, bf16[256,512]{1,0:T(8,128)(2,1)S(1)}, bf16[256,512]{1,0:T(8,128)(2,1)S(1)}, f32[256,512]{1,0:T(8,128)S(1...) custom-call(s32[2,128]{1,0:T(2,128)} %bitcast.29, ...), custom_call_target="tpu_custom_call" | custom-call | tf_op jit(solution)/shard_map/pallas_call | solution.py:219
  2.5 0.1 reshape.55
  2.6 38.2 %all_to_all.20 = bf16[128,2,384]{2,1,0:T(2,128)(2,1)S(1)} all-to-all(bf16[128,2,384]{2,1,0:T(2,128)(2,1)S(1)} %reshape.55), channel_id=1, replica_groups=mesh['z'=16,'x'=4,'core'=2,'y'=4] {'z','x','core'}, dimensions={0} | all-to-all | bytes 393216 | tf_op jit(solution)/shard_map/all_to_all | solution.py:296
  40.8 0.1 reshape.56.recv.recv1
  40.9 1.7 %shard_map.155 = (bf16[512,256]{1,0:T(8,128)(2,1)S(1)}, bf16[32,72,128]{2,1,0:T(8,128)(2,1)S(1)}) custom-call(s32[3,1,4]{2,1,0:T(1,128)S(1)} %get-tuple-element.27.index_in, bf16[256,384]{1,0:T(8,128)(2,1)S(1)} %reshape.56.recv.recv1, bf16[512,128]{1,0:T(8,128)(2,1)S(1)} %get-tuple-element.29.feat, bf16[12,128,128]{2,1,0:T(8,128)(2,1)S(1)} %get-tuple-element.30.tiles, ...), custom_call_target="tpu_custom_call" | custom-call | tf_op jit(solution)/shard_map/pallas_call | solution.py:238
  42.6 19.5 %all_to_all.21.parts = bf16[32,72,128]{2,1,0:T(8,128)(2,1)S(1)} all-to-all(bf16[32,72,128]{2,1,0:T(8,128)(2,1)S(1)} %get-tuple-element.40), channel_id=1, replica_groups=mesh['z'=16,'x'=4,'core'=2,'y'=4] {'x','core','y'}, dimensions={0} | all-to-all | bytes 1179648 | tf_op jit(solution)/shard_map/all_to_all | solution.py:296
  62.1 0.2 shard_map.156
  62.3 15.3 %all_to_all.22.parts.recv2 = bf16[16,56,128]{2,1,0:T(8,128)(2,1)S(1)} all-to-all(bf16[16,56,128]{2,1,0:T(8,128)(2,1)S(1)} %shard_map.156), channel_id=1, replica_groups=mesh['z'=16,'x'=4,'core'=2,'y'=4] {'z'}, dimensions={0} | all-to-all | bytes 458752 | tf_op jit(solution)/shard_map/all_to_all | solution.py:296
  77.6 18.8 %all_to_all.23 = bf16[32,40,128]{2,1,0:T(8,128)(2,1)S(1)} all-to-all(bf16[32,40,128]{2,1,0:T(8,128)(2,1)S(1)} %shard_map.157), channel_id=1, replica_groups=mesh['z'=16,'x'=4,'core'=2,'y'=4] {'x','core','y'}, dimensions={0} | all-to-all | bytes 655360 | tf_op jit(solution)/shard_map/all_to_all | solution.py:296
  96.5 2.0 %shard_map.158 = (bf16[172,512]{1,0:T(8,128)(2,1)}, f32[128,256]{1,0:T(8,128)}, f32[128,256]{1,0:T(8,128)}, f32[1,256]{1,0:T(1,128)}, f32[172,256]{1,0:T(8,128)}, /*index=5*/f32[172,256]{1,0:T(8,128)}) custom-call(s32[3,1,4]{2,1,0:T(1,128)S(1)} %get-tuple-element.27.index_in, bf16[1280,128]{1,0:T(8,128)(2,1)S(1)} %bitcast.22, ...), custom_call_target="tpu_custom_call" | custom-call | tf_op jit(solution)/shard_map/pallas_call | solution.py:284
  (1 shorter events, 0.0 us)
